TPU v7x, 256 devices: a whole 4x4x8 slice. The times are simulated.
256 devices in a mesh: mode: 16 (over y, z_hi), elem: 16 (over x, z_lo, core).
Axes of the slice: x: 4, y: 4, z: 8 (z_hi: 4, z_lo: 2; z = z_hi * 2 + z_lo), core: 2. Of those that a mesh axis runs over, the one named last changes fastest.
Arguments:
- velocity: bfloat16 [2, 2, 512, 81, 2048], P(None, None, 'mode', None, 'elem'), may hold values from -0.119628906 to 0.119628906
- concentration: bfloat16 [1024, 81, 2048], P(None, None, ('elem', 'mode')), may hold values from 0.049804688 to 0.546875
- stiffness: bfloat16 [4, 81, 81], replicated, may hold values from -0.625 to 0.625
- block_ids: int32 [2048], P('elem'), may hold values from 0 to 3
- radial_weight: float32 [81, 2048], P(None, 'elem'), may hold values from 0.5 to 4
Outputs:
- operator_image: float32 [2, 2, 512, 81, 2048], P(None, None, 'mode', None, 'elem')
All inputs are finite; a program needn't handle non-finite values.
Results may differ from a plain program's by a relative error of at most 0.0051.
Values may be sent and summed in bfloat16 or wider, within the bound.
No kernel may reach another device: no remote copies, remote signals or barrier semaphores. Data moves between devices by JAX's collectives and lax.ppermute only.
A program may use at most 128 MiB of HBM per device.

v0:
```python
import jax
import jax.numpy as jnp
from jax import lax
from jax.sharding import PartitionSpec as P

MODES = 512
NPHI = 1024
NODE = 81
NTYPE = 4
EZ = 16


packing_limit = 0.68
krieger_power = 1.82


def from_behind(value, axis, steps):
    count = lax.axis_size(axis)
    first, last = (max(0, -steps), min(count, count - steps))
    return lax.ppermute(value, axis, [(source, source + steps) for source in range(first, last)])


def azimuth_tables():
    planes = jnp.arange(NPHI, dtype=jnp.int32)
    orders = jnp.arange(MODES, dtype=jnp.int32)
    phase = planes[:, None] * orders[None, :] % NPHI
    angle = 2.0 * jnp.pi / NPHI * phase.astype(jnp.float32)
    weight = jnp.where(orders == 0, 1.0, 2.0).astype(jnp.float32)
    cosine = jnp.cos(angle)
    sine = jnp.sin(angle)
    inverse = jnp.concatenate([weight * cosine, -weight * sine], axis=1).astype(jnp.bfloat16)
    forward = (jnp.concatenate([cosine.T, -sine.T], axis=0) / NPHI).astype(jnp.bfloat16)
    return (inverse, forward)


def helmholtz_apply(field, ids, weight, stiffness, scale):
    total = 4.0 * scale[:, None, None] ** 2 * weight[None] * field.astype(jnp.float32)
    for block_type in range(NTYPE):
        mask = (ids == block_type).astype(jnp.float32)
        coupled = jnp.einsum(
            "ij,crmjb->crmib", stiffness[block_type], field, preferred_element_type=jnp.float32
        )
        total = total + mask * coupled
    return total


def assemble_axial(image):
    upper = image[:, :, :, :, 8]
    lower = image[:, :, :, :, 0]
    pad_high = ((0, 0),) * 5 + ((0, 1),)
    pad_low = ((0, 0),) * 5 + ((1, 0),)
    new_upper = upper + jnp.pad(lower[..., 1:], pad_high)
    new_lower = lower + jnp.pad(upper[..., :-1], pad_low)
    return image.at[:, :, :, :, 8].set(new_upper).at[:, :, :, :, 0].set(new_lower)


def body(velocity, concentration, stiffness, block_ids, radial_weight):
    local_modes = velocity.shape[2]
    elements = velocity.shape[4]
    groups = lax.axis_size("mode")
    piece = elements // groups
    inverse, forward = azimuth_tables()
    viscosity = (
        1.0 - concentration.reshape(NPHI, NODE * piece).astype(jnp.float32) / packing_limit
    ) ** (-krieger_power)
    split_field = velocity.reshape(2, 2, local_modes, NODE, groups, piece)
    gathered = lax.all_to_all(split_field, "mode", split_axis=4, concat_axis=2, tiled=True)
    comps = gathered.shape[0]
    flat_modes = gathered.reshape(comps, 2 * MODES, NODE * piece)
    physical = jnp.einsum("pk,ckn->cpn", inverse, flat_modes, preferred_element_type=jnp.float32)
    product = (viscosity[None] * physical).astype(jnp.bfloat16)
    spectral = jnp.einsum("kp,cpn->ckn", forward, product, preferred_element_type=jnp.float32)
    returned = lax.all_to_all(
        spectral.astype(jnp.bfloat16).reshape(comps, 2, MODES, NODE, 1, piece),
        "mode",
        split_axis=2,
        concat_axis=4,
        tiled=True,
    )
    spectral = returned.reshape(2, 2, local_modes, NODE, elements)
    first_mode = lax.axis_index("mode") * local_modes
    scale = (first_mode + jnp.arange(local_modes, dtype=jnp.int32)).astype(jnp.float32) / MODES
    image = helmholtz_apply(spectral, block_ids, radial_weight, stiffness, scale)
    image = assemble_axial(image.reshape(2, 2, local_modes, 9, 9, elements // EZ, EZ))
    outer = image[:, :, :, 8]
    inner = image[:, :, :, 0]
    first_inner = inner[:, :, :, :, 0]
    last_outer = outer[:, :, :, :, -1]
    from_next = from_behind(first_inner, "elem", -1)
    from_prev = from_behind(last_outer, "elem", 1)
    new_outer = outer + jnp.concatenate(
        [inner[:, :, :, :, 1:], from_next[:, :, :, :, None]], axis=4
    )
    new_inner = inner + jnp.concatenate(
        [from_prev[:, :, :, :, None], outer[:, :, :, :, :-1]], axis=4
    )
    image = image.at[:, :, :, 8].set(new_outer).at[:, :, :, 0].set(new_inner)
    return image.reshape(2, 2, local_modes, NODE, elements)


def solution(mesh):
    in_specs = (
        P(None, None, "mode", None, "elem"),
        P(None, None, ("elem", "mode")),
        P(),
        P("elem"),
        P(None, "elem"),
    )
    out_specs = P(None, None, "mode", None, "elem")
    return jax.shard_map(body, mesh=mesh, in_specs=in_specs, out_specs=out_specs, check_vma=False)
```

profile of v0, /device:TPU:70, one launch (start us, length us, event | category | flops | bytes accessed | tf_op | source)
XLA Modules:
  0.0 379.5 jit_solution(13134332266837795738)
XLA Ops:
  0.0 7.3 %copy.44 = bf16[2,2,32,81,128]{3,4,2,1,0:T(8,128)(2,1)} copy(bf16[2,2,32,81,128]{4,2,3,1,0:T(8,128)(2,1)} %param.13) | data formatting | bytes 5308416 | tf_op args[0]
  7.3 5.3 %copy.45 = bf16[2,2,32,81,16,8]{3,5,2,1,0,4:T(8,128)(2,1)} copy(bf16[2,2,32,81,16,8]{3,5,4,2,1,0:T(8,128)(2,1)} %bitcast.138) | data formatting | bytes 5308416 | tf_op jit(solution)/shard_map/reshape | solution.py:66
  12.6 10.8 %all-to-all-start = ((bf16[2,2,32,81,16,8]{3,5,2,1,0,4:T(8,128)(2,1)}), bf16[2,2,32,81,16,8]{3,5,2,1,0,4:T(8,128)(2,1)}, u32[]{:S(2)}, u32[]{:S(2)}) async-start(bf16[2,2,32,81,16,8]{3,5,2,1,0,4:T(8,128)(2,1)} %copy.45), calls=%async_computation | async-start | bytes 8388608 | tf_op jit(solution)/shard_map/all_to_all | solution.py:67
  23.4 0.0 copy-start.2
  23.4 9.2 %sine_negate_fusion = (f32[512,1024]{1,0:T(8,128)}, f32[512,1024]{1,0:T(8,128)}) fusion(), kind=kLoop, calls=%fused_computation.42 | loop fusion | flops 7864320 | bytes 4194304 | tf_op jit(solution)/shard_map/neg | solution.py:32
  32.6 0.0 copy-done.2
  32.6 3.0 power_bitcast_fusion
  35.5 9.4 %multiply_convert_fusion.1 = (bf16[1024,512]{1,0:T(8,128)(2,1)}, bf16[1024,512]{1,0:T(8,128)(2,1)}) fusion(f32[512]{0:T(512)S(1)} %fusion.34, f32[512]{0:T(512)S(1)} %fusion.33), kind=kLoop, calls=%fused_computation.45 | loop fusion | flops 9437184 | bytes 2101248 | tf_op jit(solution)/shard_map/convert.1
  44.9 73.9 %all-to-all-done = bf16[2,2,32,81,16,8]{3,5,2,1,0,4:T(8,128)(2,1)} async-done(((bf16[2,2,32,81,16,8]{3,5,2,1,0,4:T(8,128)(2,1)}), bf16[2,2,32,81,16,8]{3,5,2,1,0,4:T(8,128)(2,1)}, u32[]{:S(2)}, u32[]{:S(2)}) %all-to-all-start) | async-done | bytes 2654240 | tf_op jit(solution)/shard_map/all_to_all | solution.py:67
  118.8 20.6 %copy.46 = bf16[2,2,16,32,81,1,8]{3,2,1,6,4,0,5:T(8,128)(2,1)} copy(bf16[2,2,16,32,81,1,8]{4,6,3,1,0,2,5:T(8,128)(2,1)} %bitcast.4) | data formatting | bytes 5308416 | tf_op jit(solution)/shard_map/all_to_all | solution.py:67
  139.4 14.1 %reshape.264 = bf16[2,1024,648]{1,2,0:T(8,128)(2,1)S(1)} reshape(bf16[2,2,16,32,81,1,8]{3,2,1,6,4,0,5:T(8,128)(2,1)} %copy.46) | data formatting | bytes 5308416 | tf_op jit(solution)/shard_map/reshape | solution.py:69
  153.5 10.9 %fusion.8 = bf16[2,648,1024]{2,1,0:T(8,128)(2,1)} fusion(f32[1024,648]{0,1:T(8,128)} %power_bitcast_fusion, f32[512,1024]{1,0:T(8,128)} %get-tuple-element.66, f32[512,1024]{1,0:T(8,128)} %get-tuple-element.67, bf16[2,1024,648]{1,2,0:T(8,128)(2,1)S(1)} %reshape.264, bf16[1024,512]{1,0:T(8,128)(2,1)} %get-tuple-element.68, ...), kind=kOutput, calls=%fused_computation.29 | convolution fusion | flops 5447139328 | bytes 14254080 | tf_op jit(solution)/shard_map/kp,cpn->ckn/dot_general | solution.py:72
  164.3 8.2 %copy.47 = bf16[2,2,512,81,1,8]{3,5,1,0,4,2:T(8,128)(2,1)} copy(bf16[2,2,512,81,1,8]{2,5,1,3,0,4:T(8,128)(2,1)} %bitcast.139) | data formatting | bytes 5308416 | tf_op jit(solution)/shard_map/reshape | solution.py:74
  172.5 0.0 copy-start.5
  172.5 0.0 copy-start.3
  172.5 0.0 copy-start.4
  172.5 6.3 %all-to-all-start.1 = ((bf16[2,2,512,81,1,8]{3,5,1,0,4,2:T(8,128)(2,1)}), bf16[2,2,512,81,1,8]{3,5,1,0,4,2:T(8,128)(2,1)}, u32[]{:S(2)}, u32[]{:S(2)}) async-start(bf16[2,2,512,81,1,8]{3,5,1,0,4,2:T(8,128)(2,1)} %copy.47), calls=%async_computation.1 | async-start | bytes 8388608 | tf_op jit(solution)/shard_map/all_to_all | solution.py:73
  178.8 0.0 copy-done.5
  178.8 0.0 copy-done.3
  178.8 0.1 fusion.39
  178.9 0.0 copy-done.4
  178.9 0.2 broadcast_multiply_fusion
  179.1 95.2 %all-to-all-done.1 = bf16[2,2,512,81,1,8]{3,5,1,0,4,2:T(8,128)(2,1)} async-done(((bf16[2,2,512,81,1,8]{3,5,1,0,4,2:T(8,128)(2,1)}), bf16[2,2,512,81,1,8]{3,5,1,0,4,2:T(8,128)(2,1)}, u32[]{:S(2)}, u32[]{:S(2)}) %all-to-all-start.1) | async-done | bytes 2654240 | tf_op jit(solution)/shard_map/all_to_all | solution.py:73
  274.4 2.9 copy.48
  277.3 0.0 copy-start
  277.3 3.3 copy.98
  280.6 0.0 copy-done
  280.6 6.0 %copy.50 = bf16[2,2,32,81,128]{4,3,2,1,0:T(8,128)(2,1)} copy(bf16[2,2,32,81,128]{3,4,2,1,0:T(8,128)(2,1)} %bitcast.137) | data formatting | bytes 5308416 | tf_op jit(solution)/shard_map/reshape | solution.py:80
  286.6 0.0 copy-start.1
  286.6 5.0 %fusion.32 = f32[2,2,32,128,81]{3,4,2,1,0:T(8,128)S(1)} fusion(bf16[1,81,81]{2,0,1:T(2,128)(2,1)S(1)} %get-tuple-element.61, bf16[2,2,32,81,16,1,8]{3,6,2,4,1,0,5:T(8,128)(2,1)} %bitcast.128), kind=kOutput, calls=%fused_computation.63 | convolution fusion | flops 214990848 | bytes 7975746 | tf_op jit(solution)/shard_map/ij,crmjb->crmib/dot_general | solution.py:40
  291.6 0.0 copy-done.1
  291.6 2.6 fusion.31
  294.2 5.2 %fusion.30 = f32[2,2,32,128,81]{3,4,2,1,0:T(8,128)} fusion(bf16[1,81,81]{2,0,1:T(2,128)(2,1)S(1)} %get-tuple-element.59, bf16[2,2,32,81,16,1,8]{3,6,2,4,1,0,5:T(8,128)(2,1)S(1)} %bitcast.130), kind=kOutput, calls=%fused_computation.59 | convolution fusion | flops 214990848 | bytes 7975746 | tf_op jit(solution)/shard_map/ij,crmjb->crmib/dot_general | solution.py:40
  299.4 7.4 %bitcast_add_fusion = f32[2,2,32,81,128]{4,3,2,1,0:T(8,128)} fusion(f32[2,2,32,128,81]{3,4,2,1,0:T(8,128)} %fusion.30, f32[2,2,32,128,81]{3,4,2,1,0:T(8,128)S(1)} %fusion.31, f32[2,2,32,128,81]{3,4,2,1,0:T(8,128)S(1)} %fusion.32, bf16[2,2,32,81,128]{4,3,2,1,0:T(8,128)(2,1)} %copy.50, f32[128]{0:T(128)S(1)} %get-tuple-element.64, ...), kind=kOutput, calls=%fused_computation | convolution fusion | flops 228261888 | bytes 27884354 | tf_op jit(solution)/shard_map/ij,crmjb->crmib/dot_general | solution.py:40
  306.8 13.4 %copy.59 = f32[2,2,32,81,128]{2,4,3,1,0:T(8,128)} copy(f32[2,2,32,81,128]{4,3,2,1,0:T(8,128)} %bitcast_add_fusion) | data formatting | bytes 10616832 | tf_op jit(solution)/shard_map/add | solution.py:43
  320.2 3.0 slice_bitcast_fusion
  323.2 7.0 %copy.99 = f32[2,2,32,9,9,8,16]{2,6,5,4,3,1,0:T(8,128)S(1)} copy(f32[2,2,32,9,9,8,16]{2,6,5,4,3,1,0:T(8,128)} %bitcast.133) | data formatting | bytes 10616832
  330.2 0.2 slice.218
  330.4 0.5 bitcast_dynamic-update-slice_fusion
  330.9 2.3 bitcast_dynamic-update-slice_fusion.1
  333.2 1.0 slice_bitcast_fusion.3
  334.3 0.1 slice_bitcast_fusion.5
  334.4 0.1 slice_bitcast_fusion.4
  334.6 12.9 %collective-permute-start = (f32[2,2,32,9,16]{2,4,3,1,0:T(8,128)S(1)}, f32[2,2,32,9,16]{2,4,3,1,0:T(8,128)S(1)}, u32[]{:S(2)}, u32[]{:S(2)}) collective-permute-start(f32[2,2,32,9,16]{2,4,3,1,0:T(8,128)S(1)} %slice_bitcast_fusion.7), channel_id=1, source_target_pairs={{1,0},{2,1},{3,2},{4,3},{5,4},{6,5},{7,6},{8,7},{9,8},{10,9},{11,1... | collective-permute-start | bytes 221192 | tf_op jit(solution)/shard_map/ppermute | solution.py:20
  347.5 7.1 %copy.101 = f32[2,2,32,9,9,8,16]{2,6,5,4,3,1,0:T(8,128)} copy(f32[2,2,32,9,9,8,16]{2,6,5,4,3,1,0:T(8,128)S(1)} %bitcast_dynamic-update-slice_fusion.1) | data formatting | bytes 10616832
  354.6 1.9 collective-permute-start.1
  356.5 0.0 collective-permute-done
  356.5 1.8 fusion.6
  358.3 5.3 %collective-permute-done.1 = f32[2,2,32,9,16]{2,4,3,1,0:T(8,128)S(1)} collective-permute-done((f32[2,2,32,9,16]{2,4,3,1,0:T(8,128)S(1)}, f32[2,2,32,9,16]{2,4,3,1,0:T(8,128)S(1)}, u32[]{:S(2)}, u32[]{:S(2)}) %collective-permute-start.1) | collective-permute-done | bytes 73760 | tf_op jit(solution)/shard_map/ppermute | solution.py:20
  363.5 1.8 fusion.7
  365.3 14.2 %copy.68 = f32[2,2,32,81,128]{4,2,3,1,0:T(8,128)} copy(f32[2,2,32,81,128]{2,4,3,1,0:T(8,128)} %bitcast.135) | data formatting | bytes 10616832 | tf_op jit(solution)/shard_map/reshape | solution.py:98
  (6 shorter events, 0.1 us)
Async XLA Ops:
  12.6 106.2 %all-to-all-start = ((bf16[2,2,32,81,16,8]{3,5,2,1,0,4:T(8,128)(2,1)}), bf16[2,2,32,81,16,8]{3,5,2,1,0,4:T(8,128)(2,1)}, u32[]{:S(2)}, u32[]{:S(2)}) async-start(bf16[2,2,32,81,16,8]{3,5,2,1,0,4:T(8,128)(2,1)} %copy.45), calls=%async_computation | async-start | bytes 8388608 | tf_op jit(solution)/shard_map/all_to_all | solution.py:67
  23.4 9.2 %copy-start.2 = (bf16[1024,81,8]{0,2,1:T(8,128)(2,1)S(1)}, bf16[1024,81,8]{0,2,1:T(8,128)(2,1)}, u32[]{:S(2)}) copy-start(bf16[1024,81,8]{0,2,1:T(8,128)(2,1)} %param.14) | copy-start | bytes 3981316
  172.5 6.3 %copy-start.5 = (s32[128]{0:T(128)S(1)}, s32[128]{0:T(128)}, u32[]{:S(2)}) copy-start(s32[128]{0:T(128)} %param.16) | copy-start | bytes 1540
  172.5 6.3 %copy-start.3 = (bf16[4,81,81]{2,0,1:T(4,128)(2,1)S(1)}, bf16[4,81,81]{2,0,1:T(4,128)(2,1)}, u32[]{:S(2)}) copy-start(bf16[4,81,81]{2,0,1:T(4,128)(2,1)} %param.15) | copy-start | bytes 157468
  172.5 6.4 %copy-start.4 = (f32[81,128]{1,0:T(8,128)S(1)}, f32[81,128]{1,0:T(8,128)}, u32[]{:S(2)}) copy-start(f32[81,128]{1,0:T(8,128)} %param.17) | copy-start | bytes 124420
  172.5 101.9 %all-to-all-start.1 = ((bf16[2,2,512,81,1,8]{3,5,1,0,4,2:T(8,128)(2,1)}), bf16[2,2,512,81,1,8]{3,5,1,0,4,2:T(8,128)(2,1)}, u32[]{:S(2)}, u32[]{:S(2)}) async-start(bf16[2,2,512,81,1,8]{3,5,1,0,4,2:T(8,128)(2,1)} %copy.47), calls=%async_computation.1 | async-start | bytes 8388608 | tf_op jit(solution)/shard_map/all_to_all | solution.py:73
  277.3 3.3 copy-start
  286.6 5.0 %copy-start.1 = (bf16[2,2,512,81,1,8]{3,5,2,1,0,4:T(8,128)(2,1)S(1)}, bf16[2,2,512,81,1,8]{3,5,2,1,0,4:T(8,128)(2,1)}, u32[]{:S(2)}) copy-start(bf16[2,2,512,81,1,8]{3,5,2,1,0,4:T(8,128)(2,1)} %copy-done) | copy-start | bytes 7962628
  334.6 22.0 %collective-permute-start = (f32[2,2,32,9,16]{2,4,3,1,0:T(8,128)S(1)}, f32[2,2,32,9,16]{2,4,3,1,0:T(8,128)S(1)}, u32[]{:S(2)}, u32[]{:S(2)}) collective-permute-start(f32[2,2,32,9,16]{2,4,3,1,0:T(8,128)S(1)} %slice_bitcast_fusion.7), channel_id=1, source_target_pairs={{1,0},{2,1},{3,2},{4,3},{5,4},{6,5},{7,6},{8,7},{9,8},{10,9},{11,1... | collective-permute-start | bytes 221192 | tf_op jit(solution)/shard_map/ppermute | solution.py:20
  354.6 8.9 %collective-permute-start.1 = (f32[2,2,32,9,16]{2,4,3,1,0:T(8,128)S(1)}, f32[2,2,32,9,16]{2,4,3,1,0:T(8,128)S(1)}, u32[]{:S(2)}, u32[]{:S(2)}) collective-permute-start(f32[2,2,32,9,16]{2,4,3,1,0:T(8,128)S(1)} %slice_bitcast_fusion.6), channel_id=1, source_target_pairs={{0,1},{1,2},{2,3},{3,4},{4,5},{5,6},{6,7},{7,8},{8,9},{9,10},{10,1... | collective-permute-start | bytes 221192 | tf_op jit(solution)/shard_map/ppermute | solution.py:20
where the time goes:
time: 381 us; the launch traced here: 379 us
  waiting for transfers between devices  174 us (46%)
  local copies, waits for them, and re-layouts  114 us (30%)
  starting transfers between devices  31.9 us (8%)
  matrix products  31.1 us (8%)
  other arithmetic  28 us (7%)
    all_to_all x1, waiting for transfers between devices, body(): lax.all_to_all(spectral.astype(jnp.bfloat16).reshape(comps, 2, MODES, NOD...  95.2 us
    all_to_all x1, waiting for transfers between devices, body(): lax.all_to_all(split_field, 'mode', split_axis=4, concat_axis=2, tiled=True)  73.9 us
    unnamed x15, local copies, waits for them, and re-layouts  21.4 us
    all_to_all x1, local copies, waits for them, and re-layouts, body(): lax.all_to_all(split_field, 'mode', split_axis=4, concat_axis=2, tiled=True)  20.6 us
    dot_general x4, matrix products, helmholtz_apply(): jnp.einsum('ij,crmjb->crmib', stiffness[block_type], field, preferred_ele...  20.2 us
    ppermute x2, starting transfers between devices, from_behind(): lax.ppermute(value, axis, [(source, source + steps) for source in range(f...  14.8 us
    reshape x1, local copies, waits for them, and re-layouts, body(): return image.reshape(2, 2, local_modes, NODE, elements)  14.2 us
    reshape x1, local copies, waits for them, and re-layouts, body(): flat_modes = gathered.reshape(comps, 2 * MODES, NODE * piece)  14.1 us
  transfers between devices with their start and end apart: 4, of which 3 were waited for; matrix products, arithmetic and copies ran while one was open for 8% of the time, Pallas kernels for 0%

commit v1 on v0

v1 whole, which is shorter than its diff:
```python
import functools

import jax
import jax.numpy as jnp
from jax import lax
from jax.experimental import pallas as pl
from jax.experimental.pallas import tpu as pltpu
from jax.sharding import PartitionSpec as P

MODES = 512
NPHI = 1024
NODE = 81
EZ = 16
LANES = 128
VMEM_BYTES = 56 * 1024 * 1024

packing_limit = 0.68
krieger_power = 1.82


def params(*semantics):
    return pltpu.CompilerParams(
        vmem_limit_bytes=VMEM_BYTES, dimension_semantics=semantics or None
    )


def azimuth_tables(groups):
    planes = jnp.arange(NPHI, dtype=jnp.int32)
    orders = jnp.arange(MODES, dtype=jnp.int32)
    phase = planes[:, None] * orders[None, :] % NPHI
    angle = 2.0 * jnp.pi / NPHI * phase.astype(jnp.float32)
    weight = jnp.where(orders == 0, 1.0, 2.0).astype(jnp.float32)
    cosine = jnp.cos(angle)
    sine = jnp.sin(angle)
    inverse = jnp.stack(
        [
            (weight * cosine).T.astype(jnp.bfloat16).reshape(groups, -1, NPHI),
            (-weight * sine).T.astype(jnp.bfloat16).reshape(groups, -1, NPHI),
        ],
        axis=1,
    ).reshape(2 * MODES, NPHI)
    forward = jnp.stack(
        [
            (cosine / NPHI).astype(jnp.bfloat16).reshape(NPHI, groups, -1),
            (-sine / NPHI).astype(jnp.bfloat16).reshape(NPHI, groups, -1),
        ],
        axis=2,
    ).reshape(NPHI, 2 * MODES)
    return inverse, forward


def pack_kernel(v_ref, o_ref):
    nodes = v_ref.shape[2]
    for k in range(nodes):
        tile = v_ref[:, :, k].reshape(LANES, LANES)
        o_ref[:, k] = tile.T.reshape(o_ref.shape[0], -1, LANES)


def pack(velocity, groups, piece):
    step = 9
    modes = velocity.shape[3]
    return pl.pallas_call(
        pack_kernel,
        grid=(NODE // step,),
        in_specs=[
            pl.BlockSpec((2, 2, step, modes, LANES), lambda i: (0, 0, i, 0, 0))
        ],
        out_specs=pl.BlockSpec((groups, step, piece, LANES), lambda i: (0, i, 0, 0)),
        out_shape=jax.ShapeDtypeStruct((groups, NODE, piece, LANES), jnp.bfloat16),
        compiler_params=params("arbitrary"),
        name="pack_by_element_group",
    )(velocity)


def swap_halves(even, odd, low):
    half = LANES // 2
    return (
        jnp.where(low, even, pltpu.roll(odd, half, 1)),
        jnp.where(low, pltpu.roll(even, half, 1), odd),
    )


def azimuth_kernel(x_ref, inv_ref, fwd_ref, visc_ref, couple_ref, weight_ref, o_ref,
                   field_ref, image_ref):
    groups, rows, _ = x_ref.shape
    lane = lax.broadcasted_iota(jnp.int32, (rows, LANES), 1)
    low = lane < LANES // 2
    for t in range(groups // 2):
        first, second = swap_halves(
            x_ref[2 * t].astype(jnp.float32), x_ref[2 * t + 1].astype(jnp.float32), low
        )
        field_ref[0, :, t * LANES:(t + 1) * LANES] = first.astype(jnp.bfloat16)
        field_ref[1, :, t * LANES:(t + 1) * LANES] = second.astype(jnp.bfloat16)
    for c in range(2):
        physical = jnp.dot(field_ref[c], inv_ref[...], preferred_element_type=jnp.float32)
        product = (visc_ref[...] * physical).astype(jnp.bfloat16)
        spectral = jnp.dot(
            product, fwd_ref[...], preferred_element_type=jnp.float32
        ).astype(jnp.bfloat16)
        column = lax.broadcasted_iota(jnp.int32, (1, 2 * MODES), 1)
        order = (column // 64) * 32 + column % 32
        scale = 4.0 * (order.astype(jnp.float32) / MODES) ** 2
        image_ref[c] = jnp.dot(
            couple_ref[...], spectral, preferred_element_type=jnp.float32
        ) + (weight_ref[...] * scale) * spectral.astype(jnp.float32)
    for t in range(groups // 2):
        first, second = swap_halves(
            image_ref[0, :, t * LANES:(t + 1) * LANES],
            image_ref[1, :, t * LANES:(t + 1) * LANES],
            low,
        )
        o_ref[2 * t] = first.astype(jnp.bfloat16)
        o_ref[2 * t + 1] = second.astype(jnp.bfloat16)


def azimuth(gathered, inverse, forward, viscosity, coupling, weight):
    groups, rows, _ = gathered.shape
    return pl.pallas_call(
        azimuth_kernel,
        out_shape=jax.ShapeDtypeStruct(gathered.shape, jnp.bfloat16),
        scratch_shapes=[
            pltpu.VMEM((2, rows, 2 * MODES), jnp.bfloat16),
            pltpu.VMEM((2, rows, 2 * MODES), jnp.float32),
        ],
        compiler_params=params(),
        name="azimuth_product_and_coupling",
    )(gathered, inverse, forward, viscosity, coupling, weight)


def write_nodes(o_ref, tiles):
    lane = lax.broadcasted_iota(jnp.int32, (LANES, LANES), 1)
    place = lane % EZ
    first, last = tiles[0], tiles[8]
    tiles = list(tiles)
    tiles[8] = last + jnp.where(place < EZ - 1, pltpu.roll(first, LANES - 1, 1), 0.0)
    tiles[0] = first + jnp.where(place > 0, pltpu.roll(last, 1, 1), 0.0)
    for b in range(9):
        o_ref[:, :, b] = tiles[b].reshape(2, 2, -1, LANES)


def interior_kernel(z_ref, o_ref):
    tiles = []
    for b in range(9):
        tiles.append(z_ref[:, b].astype(jnp.float32).reshape(LANES, LANES).T)
    write_nodes(o_ref, tiles)


def face_kernel(inner_ref, outer_ref, prev_ref, next_ref, kept_ref, o_ref):
    tail = prev_ref.shape[0]

    def face(own_ref, b, before, after):
        own = own_ref[:, b].astype(jnp.float32)
        other = jnp.concatenate([before, after], axis=0).astype(jnp.float32)
        return (own + other).reshape(LANES, LANES).T

    @pl.when(pl.program_id(0) == 0)
    def _():
        write_nodes(
            o_ref,
            [face(inner_ref, b, prev_ref[:, b], outer_ref[:-tail, b]) for b in range(9)],
        )

    @pl.when(pl.program_id(0) == 1)
    def _():
        write_nodes(
            o_ref,
            [face(outer_ref, b, inner_ref[tail:, b], next_ref[:, b]) for b in range(9)],
        )


def assemble(returned, modes):
    groups, _, piece, _ = returned.shape
    faces = EZ // piece
    count = lax.axis_size("elem")
    from_next = lax.ppermute(
        returned[:faces, :9], "elem", [(e, e - 1) for e in range(1, count)]
    )
    from_prev = lax.ppermute(
        returned[-faces:, 72:], "elem", [(e, e + 1) for e in range(count - 1)]
    )
    out = jax.ShapeDtypeStruct((2, 2, NODE, modes, LANES), jnp.float32)
    block = (groups, 9, piece, LANES)
    image_block = (2, 2, 9, modes, LANES)
    image = pl.pallas_call(
        interior_kernel,
        grid=(7,),
        in_specs=[pl.BlockSpec(block, lambda i: (0, i + 1, 0, 0))],
        out_specs=pl.BlockSpec(image_block, lambda i: (0, 0, i + 1, 0, 0)),
        out_shape=out,
        compiler_params=params("arbitrary"),
        name="interior_nodes",
    )(returned)
    face_block = pl.BlockSpec((faces, 9, piece, LANES), lambda i: (0, 0, 0, 0))
    return pl.pallas_call(
        face_kernel,
        grid=(2,),
        in_specs=[
            pl.BlockSpec(block, lambda i: (0, 0, 0, 0)),
            pl.BlockSpec(block, lambda i: (0, 8, 0, 0)),
            face_block,
            face_block,
            pl.BlockSpec(memory_space=pl.ANY),
        ],
        out_specs=pl.BlockSpec(image_block, lambda i: (0, 0, 8 * i, 0, 0)),
        out_shape=out,
        input_output_aliases={4: 0},
        compiler_params=params("arbitrary"),
        name="radial_face_nodes",
    )(returned, returned, from_prev, from_next, image)


def body(velocity, concentration, stiffness, block_ids, radial_weight):
    modes = velocity.shape[2]
    elements = velocity.shape[4]
    groups = lax.axis_size("mode")
    piece = elements // groups
    rows = NODE * piece
    packed = pack(velocity.transpose(0, 1, 3, 2, 4), groups, piece)
    gathered = lax.all_to_all(
        packed.reshape(groups, rows, LANES), "mode", split_axis=0, concat_axis=0, tiled=True
    )

    inverse, forward = azimuth_tables(groups)
    viscosity = (
        1.0
        - concentration.transpose(1, 2, 0).reshape(rows, NPHI).astype(jnp.float32)
        / packing_limit
    ) ** (-krieger_power)
    first = lax.axis_index("mode") * piece
    ids = lax.dynamic_slice(block_ids, (first,), (piece,))
    weight = lax.dynamic_slice(radial_weight, (0, first), (NODE, piece)).reshape(rows, 1)
    chosen = sum(
        jnp.where((ids == kind)[None, :, None], stiffness[kind][:, None, :], 0)
        for kind in range(stiffness.shape[0])
    )
    same = jnp.eye(piece, dtype=jnp.bool_)
    coupling = jnp.where(
        same[None, :, None, :], chosen[:, :, :, None], jnp.bfloat16(0)
    ).reshape(rows, rows)

    images = azimuth(gathered, inverse, forward, viscosity, coupling, weight)
    returned = lax.all_to_all(images, "mode", split_axis=0, concat_axis=0, tiled=True)
    image = assemble(returned.reshape(groups, NODE, piece, LANES), modes)
    return image.transpose(0, 1, 3, 2, 4)


def solution(mesh):
    in_specs = (
        P(None, None, "mode", None, "elem"),
        P(None, None, ("elem", "mode")),
        P(),
        P("elem"),
        P(None, "elem"),
    )
    out_specs = P(None, None, "mode", None, "elem")
    return jax.shard_map(body, mesh=mesh, in_specs=in_specs, out_specs=out_specs, check_vma=False)
```

time: 381 us -> 183 us (0.48)
  the two profiles are of different devices: /device:TPU:70 before, /device:TPU:1 now
where the time goes in v1:
time: 183 us; the launch traced here: 182 us
  blocking collectives  60.2 us (33%)
  other arithmetic  34.4 us (19%)
  starting transfers between devices  31.4 us (17%)
  Pallas kernels  29.9 us (16%)
  local copies, waits for them, and re-layouts  23.3 us (13%)
  waiting for transfers between devices  2.34 us (1%)
    all_to_all x1, blocking collectives, body(): lax.all_to_all(images, 'mode', split_axis=0, concat_axis=0, tiled=True)  60.2 us
    ppermute x1, starting transfers between devices, assemble(): lax.ppermute(returned[-faces:, 72:], 'elem', [(e, e + 1) for e in range(c...  17.6 us
    select_n x1, local copies, waits for them, and re-layouts, body(): jnp.where(same[None, :, None, :], chosen[:, :, :, None], jnp.bfloat16(0))  15.3 us
    pallas_call x1, Pallas kernels, azimuth(): pl.pallas_call(azimuth_kernel, out_shape=jax.ShapeDtypeStruct(gathered.sh...  14.1 us
    all_to_all x1, starting transfers between devices, body(): lax.all_to_all(packed.reshape(groups, rows, LANES), 'mode', split_axis=0,...  11.9 us
    select_n x1, other arithmetic, body(): jnp.where(same[None, :, None, :], chosen[:, :, :, None], jnp.bfloat16(0))  9.62 us
    convert_element_type x1, other arithmetic, azimuth_tables(): (weight * cosine).T.astype(jnp.bfloat16).reshape(groups, -1, NPHI)  9.36 us
    convert_element_type x1, other arithmetic, azimuth_tables(): (cosine / NPHI).astype(jnp.bfloat16).reshape(NPHI, groups, -1)  9.09 us
  transfers between devices with their start and end apart: 3, of which 1 were waited for; matrix products, arithmetic and copies ran while one was open for 30% of the time, Pallas kernels for 4%

profile of v1, /device:TPU:1, one launch (start us, length us, event | category | flops | bytes accessed | tf_op | source)
XLA Modules:
  0.0 181.7 jit_solution(15815246863840965384)
XLA Ops:
  0.0 0.0 copy-start
  0.0 6.9 %pack_by_element_group.1 = bf16[16,81,8,128]{3,2,1,0:T(8,128)(2,1)} custom-call(bf16[2,2,81,32,128]{4,3,2,1,0:T(8,128)(2,1)} %bitcast.25), custom_call_target="tpu_custom_call" | custom-call | tf_op jit(solution)/shard_map/pack_by_element_group/pallas_call | solution.py:62
  6.9 0.0 copy-start.7
  6.9 0.0 copy-start.4
  6.9 11.9 %all-to-all-start = ((bf16[16,648,128]{2,1,0:T(8,128)(2,1)}), bf16[16,648,128]{2,1,0:T(8,128)(2,1)S(1)}, u32[]{:S(2)}, u32[]{:S(2)}) async-start(bf16[16,648,128]{2,1,0:T(8,128)(2,1)} %bitcast.22), calls=%async_computation | async-start | bytes 5308416 | tf_op jit(solution)/shard_map/all_to_all | solution.py:219
  18.8 0.0 copy-done.7
  18.8 0.1 broadcast_compare_fusion.3
  18.9 0.0 copy-done.4
  18.9 0.1 fusion.14
  19.1 0.2 select_add_fusion
  19.3 9.6 %broadcast_select_fusion = bf16[81,8,81,8]{3,2,1,0:T(8,128)(2,1)} fusion(pred[8,8]{1,0:T(8,128)(4,1)S(1)} %iota_compare_fusion, bf16[81,8,81]{2,1,0:T(8,128)(2,1)S(1)} %select_add_fusion), kind=kLoop, calls=%fused_computation | loop fusion | flops 419904 | bytes 944848 | tf_op jit(solution)/shard_map/jit(_where)/select_n | solution.py:237
  28.9 15.3 %select_n.100.couple_ref = bf16[648,648]{1,0:T(8,128)(2,1)} reshape(bf16[81,8,81,8]{3,2,1,0:T(8,128)(2,1)} %broadcast_select_fusion) | data formatting | bytes 1679616 | tf_op jit(solution)/shard_map/jit(_where)/select_n | solution.py:237
  44.2 0.0 copy-done
  44.2 0.1 constant_dynamic-slice_fusion
  44.3 0.9 reshape.250.weight_ref
  45.2 9.1 %multiply_convert_fusion.1 = (bf16[1024,16,1,32]{0,3,2,1:T(8,128)(2,1)S(1)}, bf16[1024,16,1,32]{0,3,2,1:T(8,128)(2,1)S(1)}) fusion(s32[16,32]{1,0:T(8,128)S(1)} %multiply_add_fusion), kind=kLoop, calls=%fused_computation.17 | loop fusion | flops 9961472 | bytes 2099200 | tf_op jit(solution)/shard_map/convert_element_type | solution.py:44
  54.3 1.5 pad_maximum_fusion.1
  55.8 3.9 %copy.11.fwd_ref = bf16[1024,1024]{1,0:T(8,128)(2,1)} copy(bf16[1024,1024]{0,1:T(8,128)(2,1)} %bitcast.24) | data formatting | bytes 4194304 | tf_op jit(solution)/shard_map/reshape | solution.py:48
  59.7 9.4 %multiply_convert_fusion.3 = (bf16[16,1,32,1024]{3,2,1,0:T(8,128)(2,1)S(1)}, bf16[16,1,32,1024]{3,2,1,0:T(8,128)(2,1)S(1)}) fusion(s32[16,32]{1,0:T(8,128)S(1)} %multiply_add_fusion, f32[16,32]{1,0:T(8,128)S(1)} %get-tuple-element.20, f32[16,32]{1,0:T(8,128)S(1)} %get-tuple-element.21), kind=kLoop, calls=%fused_computation.21 | loop fusion | flops 9437184 | bytes 2103296 | tf_op jit(solution)/shard_map/convert_element_type | solution.py:37
  69.1 0.0 copy-start.3
  69.1 1.6 pad_maximum_fusion
  70.7 0.2 copy-done.3
  70.9 3.0 %power_bitcast_fusion.visc_ref = f32[648,1024]{1,0:T(8,128)} fusion(bf16[1024,81,8]{0,2,1:T(8,128)(2,1)S(1)} %copy-done.3), kind=kLoop, calls=%fused_computation.7 | loop fusion | flops 1990656 | bytes 3981312 | tf_op jit(solution)/shard_map/pow | solution.py:224
  73.9 2.3 %all-to-all-done.x_ref = bf16[16,648,128]{2,1,0:T(8,128)(2,1)S(1)} async-done(((bf16[16,648,128]{2,1,0:T(8,128)(2,1)}), bf16[16,648,128]{2,1,0:T(8,128)(2,1)S(1)}, u32[]{:S(2)}, u32[]{:S(2)}) %all-to-all-start) | async-done | bytes 2654240 | tf_op jit(solution)/shard_map/all_to_all | solution.py:219
  76.2 0.0 copy-start.2
  76.2 1.5 copy-done.2
  77.7 14.1 %azimuth_product_and_coupling.1 = bf16[16,648,128]{2,1,0:T(8,128)(2,1)} custom-call(bf16[16,648,128]{2,1,0:T(8,128)(2,1)} %copy-done.2, bf16[1024,1024]{1,0:T(8,128)(2,1)} %bitcast.23, bf16[1024,1024]{1,0:T(8,128)(2,1)} %copy.11.fwd_ref, f32[648,1024]{1,0:T(8,128)} %power_bitcast_fusion.visc_ref, bf16[648,648]{1,0:T(8,128)(2,1)} %select_n.100.couple_ref, ...), custom_call_target="tpu_custom_call" | custom-call | tf_op jit(solution)/shard_map/azimuth_product_and_coupling/pallas_call | solution.py:118
  91.8 60.2 %all_to_all.10 = bf16[16,648,128]{2,1,0:T(8,128)(2,1)S(1)} all-to-all(bf16[16,648,128]{2,1,0:T(8,128)(2,1)} %azimuth_product_and_coupling.1), channel_id=1, replica_groups=mesh['mode'=16,'elem'=16] {'mode'}, dimensions={0} | all-to-all | bytes 5308416 | tf_op jit(solution)/shard_map/all_to_all | solution.py:242
  152.0 0.0 copy-start.1
  152.0 17.6 %collective-permute-start = (bf16[2,9,8,128]{3,2,1,0:T(8,128)(2,1)S(1)}, bf16[2,9,8,128]{3,2,1,0:T(8,128)(2,1)S(1)}, u32[]{:S(2)}, u32[]{:S(2)}) collective-permute-start(bf16[2,9,8,128]{3,2,1,0:T(8,128)(2,1)S(1)} %get-tuple-element.8), channel_id=1, source_target_pairs={{0,1},{1,2},{2,3},{3,4},{4,5},{5,6},{6,7},{7,8},{8,9},{9,10},{10,1... | collective-permute-start | bytes 110600 | tf_op jit(solution)/shard_map/ppermute | solution.py:178
  169.7 1.9 %collective-permute-start.1 = (bf16[2,9,8,128]{3,2,1,0:T(8,128)(2,1)S(1)}, bf16[2,9,8,128]{3,2,1,0:T(8,128)(2,1)S(1)}, u32[]{:S(2)}, u32[]{:S(2)}) collective-permute-start(bf16[2,9,8,128]{3,2,1,0:T(8,128)(2,1)S(1)} %get-tuple-element.7), channel_id=1, source_target_pairs={{1,0},{2,1},{3,2},{4,3},{5,4},{6,5},{7,6},{8,7},{9,8},{10,9},{11,1... | collective-permute-start | bytes 110600 | tf_op jit(solution)/shard_map/ppermute | solution.py:175
  171.6 0.0 copy-done.1
  171.6 6.4 %interior_nodes.1.kept_ref = f32[2,2,81,32,128]{4,3,2,1,0:T(8,128)} custom-call(bf16[16,81,8,128]{3,2,1,0:T(8,128)(2,1)} %bitcast.19), custom_call_target="tpu_custom_call" | custom-call | tf_op jit(solution)/shard_map/interior_nodes/pallas_call | solution.py:184
  178.0 0.0 collective-permute-done.prev_ref
  178.0 0.0 copy-start.5
  178.0 0.0 collective-permute-done.1.next_ref
  178.0 0.6 copy-done.5
  178.6 0.0 copy-start.6
  178.6 0.6 copy-done.6
  179.2 2.5 %radial_face_nodes.1 = f32[2,2,81,32,128]{4,3,2,1,0:T(8,128)} custom-call(bf16[16,81,8,128]{3,2,1,0:T(8,128)(2,1)} %bitcast.20, bf16[16,81,8,128]{3,2,1,0:T(8,128)(2,1)} %bitcast.21, bf16[2,9,8,128]{3,2,1,0:T(8,128)(2,1)} %copy-done.5, bf16[2,9,8,128]{3,2,1,0:T(8,128)(2,1)} %copy-done.6, ...), custom_call_target="tpu_custom_call", output_to_operand_aliasing={{}: (4, {})} | custom-call | tf_op jit(solution)/shard_map/radial_face_nodes/pallas_call | solution.py:194
  (7 shorter events, 0.1 us)
Async XLA Ops:
  0.0 44.2 %copy-start = (f32[81,128]{1,0:T(8,128)S(1)}, f32[81,128]{1,0:T(8,128)}, u32[]{:S(2)}) copy-start(f32[81,128]{1,0:T(8,128)} %param.9) | copy-start | bytes 124420
  6.9 11.9 %copy-start.7 = (s32[128]{0:T(128)S(1)}, s32[128]{0:T(128)}, u32[]{:S(2)}) copy-start(s32[128]{0:T(128)} %param.8) | copy-start | bytes 1540
  6.9 12.0 %copy-start.4 = (bf16[4,81,81]{2,0,1:T(4,128)(2,1)S(1)}, bf16[4,81,81]{2,0,1:T(4,128)(2,1)}, u32[]{:S(2)}) copy-start(bf16[4,81,81]{2,0,1:T(4,128)(2,1)} %param.7) | copy-start | bytes 157468
  6.9 69.3 %all-to-all-start = ((bf16[16,648,128]{2,1,0:T(8,128)(2,1)}), bf16[16,648,128]{2,1,0:T(8,128)(2,1)S(1)}, u32[]{:S(2)}, u32[]{:S(2)}) async-start(bf16[16,648,128]{2,1,0:T(8,128)(2,1)} %bitcast.22), calls=%async_computation | async-start | bytes 5308416 | tf_op jit(solution)/shard_map/all_to_all | solution.py:219
  69.1 1.8 copy-start.3
  76.2 1.5 copy-start.2
  152.0 19.6 %copy-start.1 = (bf16[16,648,128]{2,1,0:T(8,128)(2,1)}, bf16[16,648,128]{2,1,0:T(8,128)(2,1)S(1)}, u32[]{:S(2)}) copy-start(bf16[16,648,128]{2,1,0:T(8,128)(2,1)S(1)} %all_to_all.10) | copy-start | bytes 7962628
  152.0 26.0 %collective-permute-start = (bf16[2,9,8,128]{3,2,1,0:T(8,128)(2,1)S(1)}, bf16[2,9,8,128]{3,2,1,0:T(8,128)(2,1)S(1)}, u32[]{:S(2)}, u32[]{:S(2)}) collective-permute-start(bf16[2,9,8,128]{3,2,1,0:T(8,128)(2,1)S(1)} %get-tuple-element.8), channel_id=1, source_target_pairs={{0,1},{1,2},{2,3},{3,4},{4,5},{5,6},{6,7},{7,8},{8,9},{9,10},{10,1... | collective-permute-start | bytes 110600 | tf_op jit(solution)/shard_map/ppermute | solution.py:178
  169.7 8.3 %collective-permute-start.1 = (bf16[2,9,8,128]{3,2,1,0:T(8,128)(2,1)S(1)}, bf16[2,9,8,128]{3,2,1,0:T(8,128)(2,1)S(1)}, u32[]{:S(2)}, u32[]{:S(2)}) collective-permute-start(bf16[2,9,8,128]{3,2,1,0:T(8,128)(2,1)S(1)} %get-tuple-element.7), channel_id=1, source_target_pairs={{1,0},{2,1},{3,2},{4,3},{5,4},{6,5},{7,6},{8,7},{9,8},{10,9},{11,1... | collective-permute-start | bytes 110600 | tf_op jit(solution)/shard_map/ppermute | solution.py:175
  178.0 0.6 copy-start.5
  178.6 0.6 copy-start.6

commit v2 on v1

v2 whole, which is shorter than its diff:
```python
import functools

import jax
import jax.numpy as jnp
from jax import lax
from jax.experimental import pallas as pl
from jax.experimental.pallas import tpu as pltpu
from jax.sharding import PartitionSpec as P

MODES = 512
NPHI = 1024
NODE = 81
EZ = 16
LANES = 128
FACE = 9
EXTRA = 16

packing_limit = 0.68
krieger_power = 1.82


def params(mebibytes, *semantics):
    return pltpu.CompilerParams(
        vmem_limit_bytes=mebibytes * 1024 * 1024, dimension_semantics=semantics or None
    )


def azimuth_tables(groups):
    planes = jnp.arange(NPHI, dtype=jnp.int32)
    orders = jnp.arange(MODES, dtype=jnp.int32)
    phase = orders[:, None] * planes[None, :] % NPHI
    angle = 2.0 * jnp.pi / NPHI * phase.astype(jnp.float32)
    shape = (groups, MODES // groups, NPHI)
    base = jnp.stack(
        [
            jnp.cos(angle).astype(jnp.bfloat16).reshape(shape),
            (-jnp.sin(angle)).astype(jnp.bfloat16).reshape(shape),
        ],
        axis=1,
    ).reshape(2 * MODES, NPHI)
    base = lax.optimization_barrier(base)
    column = jnp.arange(2 * MODES, dtype=jnp.int32)
    weight = jnp.where(column % 32 + column // 64 == 0, 1, 2)
    inverse = base * weight.astype(jnp.bfloat16)[:, None]
    forward = base.T / jnp.bfloat16(NPHI)
    return inverse, forward


def pack_kernel(v_ref, o_ref):
    nodes = v_ref.shape[2]
    for k in range(nodes):
        tile = v_ref[:, :, k].reshape(LANES, LANES)
        o_ref[:, k] = tile.T.reshape(o_ref.shape[0], -1, LANES)


def pack(velocity, groups, piece):
    step = 27
    modes = velocity.shape[3]
    return pl.pallas_call(
        pack_kernel,
        grid=(NODE // step,),
        in_specs=[
            pl.BlockSpec((2, 2, step, modes, LANES), lambda i: (0, 0, i, 0, 0))
        ],
        out_specs=pl.BlockSpec((groups, step, piece, LANES), lambda i: (0, i, 0, 0)),
        out_shape=jax.ShapeDtypeStruct((groups, NODE, piece, LANES), jnp.bfloat16),
        compiler_params=params(58, "arbitrary"),
        name="pack_by_element_group",
    )(velocity)


def swap_halves(even, odd, low):
    half = LANES // 2
    return (
        jnp.where(low, even, pltpu.roll(odd, half, 1)),
        jnp.where(low, pltpu.roll(even, half, 1), odd),
    )


def azimuth_kernel(x_ref, inv_hbm, visc_hbm, fwd_hbm, couple_hbm, weight_ref, o_ref,
                   inv_ref, visc_ref, fwd_ref, couple_ref, field_ref, image_ref, sems):
    groups, rows, _ = x_ref.shape
    pairs = (
        (inv_hbm, inv_ref), (visc_hbm, visc_ref), (fwd_hbm, fwd_ref), (couple_hbm, couple_ref),
    )
    copies = [
        pltpu.make_async_copy(source, target, sems.at[k])
        for k, (source, target) in enumerate(pairs)
    ]
    for copy in copies:
        copy.start()
    lane = lax.broadcasted_iota(jnp.int32, (rows, LANES), 1)
    low = lane < LANES // 2
    for t in range(groups // 2):
        first, second = swap_halves(
            x_ref[2 * t].astype(jnp.float32), x_ref[2 * t + 1].astype(jnp.float32), low
        )
        field_ref[0, :, t * LANES:(t + 1) * LANES] = first.astype(jnp.bfloat16)
        field_ref[1, :, t * LANES:(t + 1) * LANES] = second.astype(jnp.bfloat16)
    for c in range(2):
        if c == 0:
            copies[0].wait()
        physical = jnp.dot(field_ref[c], inv_ref[...], preferred_element_type=jnp.float32)
        if c == 0:
            copies[1].wait()
        product = (visc_ref[...] * physical).astype(jnp.bfloat16)
        if c == 0:
            copies[2].wait()
        spectral = jnp.dot(
            product, fwd_ref[...], preferred_element_type=jnp.float32
        ).astype(jnp.bfloat16)
        column = lax.broadcasted_iota(jnp.int32, (1, 2 * MODES), 1)
        order = (column // 64) * 32 + column % 32
        scale = 4.0 * (order.astype(jnp.float32) / MODES) ** 2
        if c == 0:
            copies[3].wait()
        image_ref[c] = jnp.dot(
            couple_ref[...], spectral, preferred_element_type=jnp.float32
        ) + (weight_ref[...] * scale) * spectral.astype(jnp.float32)
    for t in range(groups // 2):
        pair = swap_halves(
            image_ref[0, :, t * LANES:(t + 1) * LANES],
            image_ref[1, :, t * LANES:(t + 1) * LANES],
            low,
        )
        for half in range(2):
            merge_axial(o_ref.at[2 * t + half], pair[half], rows // NODE)


def merge_axial(o_ref, image, piece):
    place = lax.broadcasted_iota(jnp.int32, (piece, LANES), 0)
    lowest = []
    for a in range(FACE):
        start = a * FACE * piece
        inner = image[start:start + piece]
        outer = image[start + 8 * piece:start + 9 * piece]
        outer = outer + jnp.where(place < piece - 1, pltpu.roll(inner, piece - 1, 0), 0.0)
        kept = image[start + piece:start + 8 * piece]
        o_ref[a * 8 * piece:(a + 1) * 8 * piece] = jnp.concatenate(
            [kept, outer], axis=0
        ).astype(jnp.bfloat16)
        lowest.append(inner[:1])
    lowest.append(jnp.zeros((EXTRA - FACE, LANES), jnp.float32))
    o_ref[FACE * 8 * piece:] = jnp.concatenate(lowest, axis=0).astype(jnp.bfloat16)


def azimuth(gathered, inverse, viscosity, forward, coupling, weight):
    groups, rows, _ = gathered.shape
    sent = FACE * 8 * (rows // NODE) + EXTRA
    vmem = pl.BlockSpec(memory_space=pltpu.VMEM)
    hbm = pl.BlockSpec(memory_space=pltpu.HBM)
    held = [
        pltpu.with_memory_space_constraint(value, pltpu.HBM)
        for value in (inverse, viscosity, forward, coupling)
    ]
    return pl.pallas_call(
        azimuth_kernel,
        in_specs=[vmem, hbm, hbm, hbm, hbm, vmem],
        out_specs=vmem,
        out_shape=jax.ShapeDtypeStruct((groups, sent, LANES), jnp.bfloat16),
        scratch_shapes=[pltpu.VMEM(value.shape, value.dtype) for value in held] + [
            pltpu.VMEM((2, rows, 2 * MODES), jnp.bfloat16),
            pltpu.VMEM((2, rows, 2 * MODES), jnp.float32),
            pltpu.SemaphoreType.DMA((len(held),)),
        ],
        compiler_params=params(40),
        name="azimuth_product_and_coupling",
    )(gathered, *held, weight)


def lowest_nodes(values):
    groups = values.shape[0]
    return jnp.broadcast_to(
        values[:, None, :], (groups, LANES // groups, LANES)
    ).reshape(LANES, LANES)


def row_of(extra, a):
    place = lax.broadcasted_iota(jnp.int32, extra.shape, 1)
    return jnp.sum(jnp.where(place == a, extra, 0.0), axis=1)


def write_nodes(o_ref, image, lowest):
    groups, rows, _ = image.shape
    piece = rows // 8
    place = lax.broadcasted_iota(jnp.int32, (LANES, LANES), 1) % EZ
    zero = lowest_nodes(lowest).T
    tiles = []
    for b in range(8):
        tiles.append(image[:, b * piece:(b + 1) * piece].reshape(LANES, LANES).T)
    crossing = (place % piece == piece - 1) & (place < EZ - 1)
    tiles[7] = tiles[7] + jnp.where(crossing, pltpu.roll(zero, LANES - 1, 1), 0.0)
    tiles.insert(0, jnp.where(place == 0, zero, pltpu.roll(tiles[7], 1, 1)))
    for b in range(FACE):
        o_ref[:, :, b] = tiles[b].reshape(2, 2, -1, LANES)


def interior_kernel(z_ref, extra_ref, o_ref):
    a = pl.program_id(0) + 1
    write_nodes(
        o_ref,
        z_ref[...].astype(jnp.float32),
        row_of(extra_ref[...].astype(jnp.float32), a),
    )


def face_kernel(inner_ref, outer_ref, extra_ref, prev_ref, next_ref, kept_ref, o_ref):
    tail = prev_ref.shape[0]
    rows = inner_ref.shape[1]
    wide = lambda value: value.astype(jnp.float32)
    extra = wide(extra_ref[...])

    @pl.when(pl.program_id(0) == 0)
    def _():
        far = wide(prev_ref[...])
        other = jnp.concatenate([far[:, :rows], wide(outer_ref[:-tail])], axis=0)
        ends = jnp.concatenate([row_of(far[:, rows:], 8), row_of(extra[:-tail], 8)], axis=0)
        write_nodes(o_ref, wide(inner_ref[...]) + other, row_of(extra, 0) + ends)

    @pl.when(pl.program_id(0) == 1)
    def _():
        far = wide(next_ref[...])
        other = jnp.concatenate([wide(inner_ref[tail:]), far[:, :rows]], axis=0)
        ends = jnp.concatenate([row_of(extra[tail:], 0), row_of(far[:, rows:], 0)], axis=0)
        write_nodes(o_ref, wide(outer_ref[...]) + other, row_of(extra, 8) + ends)


def assemble(returned, modes, piece):
    groups = returned.shape[0]
    rows = 8 * piece
    faces = EZ // piece
    count = lax.axis_size("elem")
    inner = jnp.concatenate([returned[:faces, :rows], returned[:faces, -EXTRA:]], axis=1)
    outer = jnp.concatenate(
        [returned[-faces:, 8 * rows:9 * rows], returned[-faces:, -EXTRA:]], axis=1
    )
    from_next = lax.ppermute(inner, "elem", [(e, e - 1) for e in range(1, count)])
    from_prev = lax.ppermute(outer, "elem", [(e, e + 1) for e in range(count - 1)])
    out = jax.ShapeDtypeStruct((2, 2, NODE, modes, LANES), jnp.float32)
    block = (groups, rows, LANES)
    extra_block = pl.BlockSpec(
        (groups, EXTRA, LANES), lambda i: (0, FACE * rows // EXTRA, 0)
    )
    image_block = (2, 2, FACE, modes, LANES)
    image = pl.pallas_call(
        interior_kernel,
        grid=(7,),
        in_specs=[pl.BlockSpec(block, lambda i: (0, i + 1, 0)), extra_block],
        out_specs=pl.BlockSpec(image_block, lambda i: (0, 0, i + 1, 0, 0)),
        out_shape=out,
        compiler_params=params(12, "arbitrary"),
        name="interior_nodes",
    )(returned, returned)
    face_block = pl.BlockSpec(from_prev.shape, lambda i: (0, 0, 0))
    return pl.pallas_call(
        face_kernel,
        grid=(2,),
        in_specs=[
            pl.BlockSpec(block, lambda i: (0, 0, 0)),
            pl.BlockSpec(block, lambda i: (0, 8, 0)),
            extra_block,
            face_block,
            face_block,
            pl.BlockSpec(memory_space=pl.ANY),
        ],
        out_specs=pl.BlockSpec(image_block, lambda i: (0, 0, 8 * i, 0, 0)),
        out_shape=out,
        input_output_aliases={5: 0},
        compiler_params=params(12, "arbitrary"),
        name="radial_face_nodes",
    )(returned, returned, returned, from_prev, from_next, image)


def body(velocity, concentration, stiffness, block_ids, radial_weight):
    modes = velocity.shape[2]
    elements = velocity.shape[4]
    groups = lax.axis_size("mode")
    piece = elements // groups
    rows = NODE * piece
    packed = pack(velocity.transpose(0, 1, 3, 2, 4), groups, piece)
    gathered = lax.all_to_all(
        packed.reshape(groups, rows, LANES), "mode", split_axis=0, concat_axis=0, tiled=True
    )

    inverse, forward = azimuth_tables(groups)
    viscosity = (
        1.0
        - concentration.transpose(1, 2, 0).reshape(rows, NPHI).astype(jnp.float32)
        / packing_limit
    ) ** (-krieger_power)
    first = lax.axis_index("mode") * piece
    ids = lax.dynamic_slice(block_ids, (first,), (piece,))
    weight = lax.dynamic_slice(radial_weight, (0, first), (NODE, piece)).reshape(rows, 1)
    row = jnp.arange(rows, dtype=jnp.int32)
    spread = (row[:, None] // piece == jnp.arange(NODE)[None, :]).astype(jnp.bfloat16)
    ids = jnp.tile(ids, NODE)
    kinds = jnp.einsum("ni,tij->tnj", spread, stiffness, preferred_element_type=jnp.bfloat16)
    chosen = jnp.zeros((rows, NODE), jnp.bfloat16)
    for kind in range(stiffness.shape[0]):
        chosen = jnp.where((ids == kind)[:, None], kinds[kind], chosen)
    coupling = jnp.where(
        row[:, None] % piece == row[None, :] % piece,
        jnp.einsum("nj,mj->nm", chosen, spread, preferred_element_type=jnp.bfloat16),
        jnp.bfloat16(0),
    )

    images = azimuth(gathered, inverse, viscosity, forward, coupling, weight)
    returned = lax.all_to_all(images, "mode", split_axis=0, concat_axis=0, tiled=True)
    image = assemble(returned, modes, piece)
    return image.transpose(0, 1, 3, 2, 4)


def solution(mesh):
    in_specs = (
        P(None, None, "mode", None, "elem"),
        P(None, None, ("elem", "mode")),
        P(),
        P("elem"),
        P(None, "elem"),
    )
    out_specs = P(None, None, "mode", None, "elem")
    return jax.shard_map(body, mesh=mesh, in_specs=in_specs, out_specs=out_specs, check_vma=False)
```

time: 183 us -> 167 us (0.913)
  waiting for transfers between devices: 2.34 us -> 33.4 us
  local copies, waits for them, and re-layouts: 23.3 us -> 5.43 us
  other arithmetic: 34.4 us -> 16.7 us
  Pallas kernels: 29.9 us -> 22.5 us
  blocking collectives: 60.2 us -> 55.2 us
    all_to_all x1, waiting for transfers between devices: 2.34 us -> 33.4 us  [body(): lax.all_to_all(packed.reshape(groups, rows, LANES), 'mode', split_axis=0,...]
    select_n x1 -> x0, local copies, waits for them, and re-layouts: 15.3 us -> none  [body(): jnp.where(same[None, :, None, :], chosen[:, :, :, None], jnp.bfloat16(0))]
    select_n x2 -> x1, other arithmetic: 9.63 us -> 0.01 us  [body(): row[:, None] // piece == jnp.arange(NODE)[None, :]]
    convert_element_type x2, other arithmetic: 18.4 us -> 9.05 us  [the longest x1 9.05 us: azimuth_tables(): jnp.cos(angle).astype(jnp.bfloat16).reshape(shape)]
    all_to_all x1, blocking collectives: 60.2 us -> 55.2 us  [body(): lax.all_to_all(images, 'mode', split_axis=0, concat_axis=0, tiled=True)]
    optimization_barrier x0 -> x1, local copies, waits for them, and re-layouts: none -> 3.94 us  [azimuth_tables(): base = lax.optimization_barrier(base)]
    reshape x1 -> x0, local copies, waits for them, and re-layouts: 3.92 us -> none  [azimuth_tables(): forward = jnp.stack([(cosine / NPHI).astype(jnp.bfloat16).reshape(NPHI, g...]
    pallas_call x1, Pallas kernels: 14.1 us -> 11.6 us  [azimuth(): pl.pallas_call(azimuth_kernel, in_specs=[vmem, hbm, hbm, hbm, hbm, vmem],...]
  transfers between devices with their start and end apart: 3 -> 3, of which waited for: 1 -> 1; matrix products, arithmetic and copies ran while one was open for 30% -> 14% of each run, Pallas kernels for 4% -> 3%
where the time goes in v2:
time: 167 us; the launch traced here: 166 us
  blocking collectives  55.2 us (33%)
  waiting for transfers between devices  33.4 us (20%)
  starting transfers between devices  30.9 us (19%)
  Pallas kernels  22.5 us (13%)
  other arithmetic  16.7 us (10%)
  local copies, waits for them, and re-layouts  5.43 us (3%)
  matrix products  1.79 us (1%)
    all_to_all x1, blocking collectives, body(): lax.all_to_all(images, 'mode', split_axis=0, concat_axis=0, tiled=True)  55.2 us
    all_to_all x1, waiting for transfers between devices, body(): lax.all_to_all(packed.reshape(groups, rows, LANES), 'mode', split_axis=0,...  33.4 us
    ppermute x1, starting transfers between devices, assemble(): lax.ppermute(outer, 'elem', [(e, e + 1) for e in range(count - 1)])  17.1 us
    all_to_all x1, starting transfers between devices, body(): lax.all_to_all(packed.reshape(groups, rows, LANES), 'mode', split_axis=0,...  11.9 us
    pallas_call x1, Pallas kernels, azimuth(): pl.pallas_call(azimuth_kernel, in_specs=[vmem, hbm, hbm, hbm, hbm, vmem],...  11.6 us
    convert_element_type x1, other arithmetic, azimuth_tables(): jnp.cos(angle).astype(jnp.bfloat16).reshape(shape)  9.05 us
    pallas_call x1, Pallas kernels, assemble(): pl.pallas_call(interior_kernel, grid=(7,), in_specs=[pl.BlockSpec(block,...  4.64 us
    pallas_call x1, Pallas kernels, pack(): pl.pallas_call(pack_kernel, grid=(NODE // step,), in_specs=[pl.BlockSpec(...  4.51 us
  transfers between devices with their start and end apart: 3, of which 1 were waited for; matrix products, arithmetic and copies ran while one was open for 14% of the time, Pallas kernels for 3%

profile of v2, /device:TPU:1, one launch (start us, length us, event | category | flops | bytes accessed | tf_op | source)
XLA Modules:
  0.0 166.1 jit_solution(13454955766344391404)
XLA Ops:
  0.0 0.0 copy-start
  0.0 4.5 %pack_by_element_group.1 = bf16[16,81,8,128]{3,2,1,0:T(8,128)(2,1)} custom-call(bf16[2,2,81,32,128]{4,3,2,1,0:T(8,128)(2,1)} %bitcast.44), custom_call_target="tpu_custom_call" | custom-call | tf_op jit(solution)/shard_map/pack_by_element_group/pallas_call | solution.py:59
  4.5 0.0 copy-start.5
  4.5 0.0 copy-start.4
  4.5 11.9 %all-to-all-start = ((bf16[16,648,128]{2,1,0:T(8,128)(2,1)}), bf16[16,648,128]{2,1,0:T(8,128)(2,1)S(1)}, u32[]{:S(2)}, u32[]{:S(2)}) async-start(bf16[16,648,128]{2,1,0:T(8,128)(2,1)} %bitcast.43), calls=%async_computation | async-start | bytes 5308416 | tf_op jit(solution)/shard_map/all_to_all | solution.py:281
  16.4 0.0 copy-done.5
  16.4 0.1 broadcast_compare_fusion.3
  16.5 0.1 eq.115
  16.6 0.1 eq.108
  16.8 0.1 eq.117
  16.9 0.1 eq.119
  17.0 0.0 copy-done.4
  17.0 0.1 constant_dynamic-slice_fusion
  17.1 0.2 reshape.223.weight_ref
  17.2 9.0 %cosine_convert_fusion = (bf16[16,1,32,1024]{3,2,1,0:T(8,128)(2,1)S(1)}, bf16[16,1,32,1024]{3,2,1,0:T(8,128)(2,1)S(1)}) fusion(s32[16,32]{1,0:T(8,128)S(1)} %multiply_add_fusion), kind=kLoop, calls=%fused_computation.10 | loop fusion | flops 8912896 | bytes 2099200 | tf_op jit(solution)/shard_map/convert_element_type | solution.py:36
  26.3 1.5 pad_maximum_fusion
  27.8 3.9 %copy.9 = bf16[1024,1024]{0,1:T(8,128)(2,1)} copy(bf16[1024,1024]{1,0:T(8,128)(2,1)} %bitcast.41) | data formatting | bytes 4194304 | tf_op jit(solution)/shard_map/optimization_barrier | solution.py:41
  31.8 0.0 copy-start.3
  31.8 0.0 copy-done
  31.8 0.3 convolution_bitcast_fusion
  32.1 1.5 compare_select_fusion.couple_hbm
  33.6 0.0 copy-done.3
  33.6 0.0 copy-start.2
  33.6 3.0 %power_bitcast_fusion.visc_hbm = f32[648,1024]{1,0:T(8,128)} fusion(bf16[1024,81,8]{0,2,1:T(8,128)(2,1)S(1)} %copy-done.3), kind=kLoop, calls=%fused_computation.3 | loop fusion | flops 1990656 | bytes 3981312 | tf_op jit(solution)/shard_map/pow | solution.py:286
  36.6 0.0 copy-done.2
  36.6 0.0 copy-start.1
  36.6 1.5 multiply_bitcast_fusion.fwd_hbm
  38.1 0.8 copy-done.1
  38.9 1.5 broadcast_multiply_fusion.inv_hbm
  40.5 33.4 %all-to-all-done.x_ref = bf16[16,648,128]{2,1,0:T(8,128)(2,1)S(1)} async-done(((bf16[16,648,128]{2,1,0:T(8,128)(2,1)}), bf16[16,648,128]{2,1,0:T(8,128)(2,1)S(1)}, u32[]{:S(2)}, u32[]{:S(2)}) %all-to-all-start) | async-done | bytes 2654240 | tf_op jit(solution)/shard_map/all_to_all | solution.py:281
  73.8 11.6 %azimuth_product_and_coupling.1 = bf16[16,592,128]{2,1,0:T(8,128)(2,1)S(1)} custom-call(bf16[16,648,128]{2,1,0:T(8,128)(2,1)S(1)} %all-to-all-done.x_ref, bf16[1024,1024]{1,0:T(8,128)(2,1)} %broadcast_multiply_fusion.inv_hbm, f32[648,1024]{1,0:T(8,128)} %power_bitcast_fusion.visc_hbm, bf16[1024,1024]{1,0:T(8,128)(2,1)} %multiply_bitcast_fusion.fwd_hbm, ...), custom_call_target="tpu_custom_call" | custom-call | tf_op jit(solution)/shard_map/azimuth_product_and_coupling/pallas_call | solution.py:156
  85.5 55.2 %all_to_all.10.z_ref.extra_ref.inner_ref.outer_ref = bf16[16,592,128]{2,1,0:T(8,128)(2,1)S(1)} all-to-all(bf16[16,592,128]{2,1,0:T(8,128)(2,1)S(1)} %azimuth_product_and_coupling.1), channel_id=1, replica_groups=mesh['mode'=16,'elem'=16] {'mode'}, dimensions={0} | all-to-all | bytes 4849664 | tf_op jit(solution)/shard_map/all_to_all | solution.py:308
  140.7 17.1 %collective-permute-start = (bf16[2,80,128]{2,1,0:T(8,128)(2,1)S(1)}, bf16[2,80,128]{2,1,0:T(8,128)(2,1)S(1)}, u32[]{:S(2)}, u32[]{:S(2)}) collective-permute-start(bf16[2,80,128]{2,1,0:T(8,128)(2,1)S(1)} %concatenate.8), channel_id=1, source_target_pairs={{0,1},{1,2},{2,3},{3,4},{4,5},{5,6},{6,7},{7,8},{8,9},{9,10},{10,1... | collective-permute-start | bytes 122888 | tf_op jit(solution)/shard_map/ppermute | solution.py:238
  157.8 1.9 %collective-permute-start.1 = (bf16[2,80,128]{2,1,0:T(8,128)(2,1)S(1)}, bf16[2,80,128]{2,1,0:T(8,128)(2,1)S(1)}, u32[]{:S(2)}, u32[]{:S(2)}) collective-permute-start(bf16[2,80,128]{2,1,0:T(8,128)(2,1)S(1)} %pad_maximum_fusion.1), channel_id=1, source_target_pairs={{1,0},{2,1},{3,2},{4,3},{5,4},{6,5},{7,6},{8,7},{9,8},{10,9},{11,1... | collective-permute-start | bytes 122888 | tf_op jit(solution)/shard_map/ppermute | solution.py:237
  159.7 4.6 %interior_nodes.1.kept_ref = f32[2,2,81,32,128]{4,3,2,1,0:T(8,128)} custom-call(bf16[16,592,128]{2,1,0:T(8,128)(2,1)S(1)} %all_to_all.10.z_ref.extra_ref.inner_ref.outer_ref, bf16[16,592,128]{2,1,0:T(8,128)(2,1)S(1)} %all_to_all.10.z_ref.extra_ref.inner_ref.outer_ref), custom_call_target="tpu_custom_call" | custom-call | tf_op jit(solution)/shard_map/interior_nodes/pallas_call | solution.py:245
  164.4 0.0 collective-permute-done.prev_ref
  164.4 0.0 collective-permute-done.1.next_ref
  164.4 1.7 %radial_face_nodes.1 = f32[2,2,81,32,128]{4,3,2,1,0:T(8,128)} custom-call(bf16[16,592,128]{2,1,0:T(8,128)(2,1)S(1)} %all_to_all.10.z_ref.extra_ref.inner_ref.outer_ref, bf16[16,592,128]{2,1,0:T(8,128)(2,1)S(1)} %all_to_all.10.z_ref.extra_ref.inner_ref.outer_ref, ...), custom_call_target="tpu_custom_call", output_to_operand_aliasing={{}: (5, {})} | custom-call | tf_op jit(solution)/shard_map/radial_face_nodes/pallas_call | solution.py:255
  (12 shorter events, 0.1 us)
Async XLA Ops:
  0.0 31.8 %copy-start = (bf16[4,81,81]{2,0,1:T(4,128)(2,1)S(1)}, bf16[4,81,81]{2,0,1:T(4,128)(2,1)}, u32[]{:S(2)}) copy-start(bf16[4,81,81]{2,0,1:T(4,128)(2,1)} %param.7) | copy-start | bytes 157468
  4.5 11.9 %copy-start.5 = (s32[128]{0:T(128)S(1)}, s32[128]{0:T(128)}, u32[]{:S(2)}) copy-start(s32[128]{0:T(128)} %param.8) | copy-start | bytes 1540
  4.5 12.4 %copy-start.4 = (f32[81,128]{1,0:T(8,128)S(1)}, f32[81,128]{1,0:T(8,128)}, u32[]{:S(2)}) copy-start(f32[81,128]{1,0:T(8,128)} %param.9) | copy-start | bytes 124420
  4.5 69.3 %all-to-all-start = ((bf16[16,648,128]{2,1,0:T(8,128)(2,1)}), bf16[16,648,128]{2,1,0:T(8,128)(2,1)S(1)}, u32[]{:S(2)}, u32[]{:S(2)}) async-start(bf16[16,648,128]{2,1,0:T(8,128)(2,1)} %bitcast.43), calls=%async_computation | async-start | bytes 5308416 | tf_op jit(solution)/shard_map/all_to_all | solution.py:281
  31.8 1.8 %copy-start.3 = (bf16[1024,81,8]{0,2,1:T(8,128)(2,1)S(1)}, bf16[1024,81,8]{0,2,1:T(8,128)(2,1)}, u32[]{:S(2)}) copy-start(bf16[1024,81,8]{0,2,1:T(8,128)(2,1)} %param.6) | copy-start | bytes 3981316
  33.6 3.0 %copy-start.2 = (bf16[1024,1024]{0,1:T(8,128)(2,1)S(1)}, bf16[1024,1024]{0,1:T(8,128)(2,1)}, u32[]{:S(2)}) copy-start(bf16[1024,1024]{0,1:T(8,128)(2,1)} %copy.9) | copy-start | bytes 6291460
  36.6 2.3 %copy-start.1 = (bf16[16,2,32,1024]{3,2,1,0:T(8,128)(2,1)S(1)}, bf16[16,2,32,1024]{3,2,1,0:T(8,128)(2,1)}, u32[]{:S(2)}) copy-start(bf16[16,2,32,1024]{3,2,1,0:T(8,128)(2,1)} %pad_maximum_fusion) | copy-start | bytes 6291460
  140.7 23.7 %collective-permute-start = (bf16[2,80,128]{2,1,0:T(8,128)(2,1)S(1)}, bf16[2,80,128]{2,1,0:T(8,128)(2,1)S(1)}, u32[]{:S(2)}, u32[]{:S(2)}) collective-permute-start(bf16[2,80,128]{2,1,0:T(8,128)(2,1)S(1)} %concatenate.8), channel_id=1, source_target_pairs={{0,1},{1,2},{2,3},{3,4},{4,5},{5,6},{6,7},{7,8},{8,9},{9,10},{10,1... | collective-permute-start | bytes 122888 | tf_op jit(solution)/shard_map/ppermute | solution.py:238
  157.8 6.6 %collective-permute-start.1 = (bf16[2,80,128]{2,1,0:T(8,128)(2,1)S(1)}, bf16[2,80,128]{2,1,0:T(8,128)(2,1)S(1)}, u32[]{:S(2)}, u32[]{:S(2)}) collective-permute-start(bf16[2,80,128]{2,1,0:T(8,128)(2,1)S(1)} %pad_maximum_fusion.1), channel_id=1, source_target_pairs={{1,0},{2,1},{3,2},{4,3},{5,4},{6,5},{7,6},{8,7},{9,8},{10,9},{11,1... | collective-permute-start | bytes 122888 | tf_op jit(solution)/shard_map/ppermute | solution.py:237

commit v3 on v2

--- a/solution.py
+++ b/solution.py
@@ -14,6 +14,7 @@
 LANES = 128
 FACE = 9
 EXTRA = 16
+STAGES = (3, 5, 7)
 
 packing_limit = 0.68
 krieger_power = 1.82
@@ -46,27 +47,50 @@
     return inverse, forward
 
 
-def pack_kernel(v_ref, o_ref):
-    nodes = v_ref.shape[2]
-    for k in range(nodes):
-        tile = v_ref[:, :, k].reshape(LANES, LANES)
-        o_ref[:, k] = tile.T.reshape(o_ref.shape[0], -1, LANES)
+PACK_STEP = 9
+
+
+def pack_kernel(v_hbm, o_hbm, v_ref, o_ref, v_sems, o_sems):
+    steps = NODE // PACK_STEP
+    nodes = [pl.ds(i * PACK_STEP, PACK_STEP) for i in range(steps)]
+    arrivals = [
+        pltpu.make_async_copy(v_hbm.at[:, :, nodes[i]], v_ref.at[:, :, nodes[i]], v_sems.at[i])
+        for i in range(steps)
+    ]
+    departures = [
+        pltpu.make_async_copy(o_ref.at[:, nodes[i]], o_hbm.at[:, nodes[i]], o_sems.at[i])
+        for i in range(steps)
+    ]
+    for copy in arrivals:
+        copy.start()
+    for i in range(steps):
+        arrivals[i].wait()
+        for k in range(i * PACK_STEP, (i + 1) * PACK_STEP):
+            tile = v_ref[:, :, k].reshape(LANES, LANES)
+            o_ref[:, k] = tile.T.reshape(o_ref.shape[0], -1, LANES)
+        departures[i].start()
+    for copy in departures:
+        copy.wait()
 
 
 def pack(velocity, groups, piece):
-    step = 27
-    modes = velocity.shape[3]
+    steps = NODE // PACK_STEP
+    hbm = pl.BlockSpec(memory_space=pltpu.HBM)
+    packed = (groups, NODE, piece, LANES)
     return pl.pallas_call(
         pack_kernel,
-        grid=(NODE // step,),
-        in_specs=[
-            pl.BlockSpec((2, 2, step, modes, LANES), lambda i: (0, 0, i, 0, 0))
+        in_specs=[hbm],
+        out_specs=hbm,
+        out_shape=jax.ShapeDtypeStruct(packed, jnp.bfloat16),
+        scratch_shapes=[
+            pltpu.VMEM(velocity.shape, jnp.bfloat16),
+            pltpu.VMEM(packed, jnp.bfloat16),
+            pltpu.SemaphoreType.DMA((steps,)),
+            pltpu.SemaphoreType.DMA((steps,)),
         ],
-        out_specs=pl.BlockSpec((groups, step, piece, LANES), lambda i: (0, i, 0, 0)),
-        out_shape=jax.ShapeDtypeStruct((groups, NODE, piece, LANES), jnp.bfloat16),
-        compiler_params=params(58, "arbitrary"),
+        compiler_params=params(58),
         name="pack_by_element_group",
-    )(velocity)
+    )(pltpu.with_memory_space_constraint(velocity, pltpu.HBM))
 
 
 def swap_halves(even, odd, low):
@@ -87,8 +111,7 @@
         pltpu.make_async_copy(source, target, sems.at[k])
         for k, (source, target) in enumerate(pairs)
     ]
-    for copy in copies:
-        copy.start()
+    copies[0].start()
     lane = lax.broadcasted_iota(jnp.int32, (rows, LANES), 1)
     low = lane < LANES // 2
     for t in range(groups // 2):
@@ -97,6 +120,8 @@
         )
         field_ref[0, :, t * LANES:(t + 1) * LANES] = first.astype(jnp.bfloat16)
         field_ref[1, :, t * LANES:(t + 1) * LANES] = second.astype(jnp.bfloat16)
+        if t in STAGES:
+            copies[STAGES.index(t) + 1].start()
     for c in range(2):
         if c == 0:
             copies[0].wait()
@@ -204,24 +229,25 @@
     )
 
 
-def face_kernel(inner_ref, outer_ref, extra_ref, prev_ref, next_ref, kept_ref, o_ref):
-    tail = prev_ref.shape[0]
+def face_kernel(odd_ref, inner_ref, outer_ref, extra_ref, near_ref, far_ref, kept_ref, o_ref):
+    tail = near_ref.shape[1]
     rows = inner_ref.shape[1]
+    odd = odd_ref[0] == 1
     wide = lambda value: value.astype(jnp.float32)
     extra = wide(extra_ref[...])
 
     @pl.when(pl.program_id(0) == 0)
     def _():
-        far = wide(prev_ref[...])
-        other = jnp.concatenate([far[:, :rows], wide(outer_ref[:-tail])], axis=0)
-        ends = jnp.concatenate([row_of(far[:, rows:], 8), row_of(extra[:-tail], 8)], axis=0)
+        prev = jnp.where(odd, wide(near_ref[1]), wide(far_ref[1]))
+        other = jnp.concatenate([prev[:, :rows], wide(outer_ref[:-tail])], axis=0)
+        ends = jnp.concatenate([row_of(prev[:, rows:], 8), row_of(extra[:-tail], 8)], axis=0)
         write_nodes(o_ref, wide(inner_ref[...]) + other, row_of(extra, 0) + ends)
 
     @pl.when(pl.program_id(0) == 1)
     def _():
-        far = wide(next_ref[...])
-        other = jnp.concatenate([wide(inner_ref[tail:]), far[:, :rows]], axis=0)
-        ends = jnp.concatenate([row_of(extra[tail:], 0), row_of(far[:, rows:], 0)], axis=0)
+        after = jnp.where(odd, wide(far_ref[0]), wide(near_ref[0]))
+        other = jnp.concatenate([wide(inner_ref[tail:]), after[:, :rows]], axis=0)
+        ends = jnp.concatenate([row_of(extra[tail:], 0), row_of(after[:, rows:], 0)], axis=0)
         write_nodes(o_ref, wide(outer_ref[...]) + other, row_of(extra, 8) + ends)
 
 
@@ -234,8 +260,10 @@
     outer = jnp.concatenate(
         [returned[-faces:, 8 * rows:9 * rows], returned[-faces:, -EXTRA:]], axis=1
     )
-    from_next = lax.ppermute(inner, "elem", [(e, e - 1) for e in range(1, count)])
-    from_prev = lax.ppermute(outer, "elem", [(e, e + 1) for e in range(count - 1)])
+    both = jnp.stack([inner, outer])
+    near = lax.ppermute(both, "elem", [(e, e ^ 1) for e in range(count)])
+    far = lax.ppermute(both, "elem", [(e, ((e + 1) ^ 1) - 1) for e in range(1, count - 1)])
+    odd = (lax.axis_index("elem") % 2).reshape(1)
     out = jax.ShapeDtypeStruct((2, 2, NODE, modes, LANES), jnp.float32)
     block = (groups, rows, LANES)
     extra_block = pl.BlockSpec(
@@ -251,11 +279,12 @@
         compiler_params=params(12, "arbitrary"),
         name="interior_nodes",
     )(returned, returned)
-    face_block = pl.BlockSpec(from_prev.shape, lambda i: (0, 0, 0))
+    face_block = pl.BlockSpec(both.shape, lambda i: (0, 0, 0, 0))
     return pl.pallas_call(
         face_kernel,
         grid=(2,),
         in_specs=[
+            pl.BlockSpec(memory_space=pltpu.SMEM),
             pl.BlockSpec(block, lambda i: (0, 0, 0)),
             pl.BlockSpec(block, lambda i: (0, 8, 0)),
             extra_block,
@@ -265,10 +294,10 @@
         ],
         out_specs=pl.BlockSpec(image_block, lambda i: (0, 0, 8 * i, 0, 0)),
         out_shape=out,
-        input_output_aliases={5: 0},
+        input_output_aliases={6: 0},
         compiler_params=params(12, "arbitrary"),
         name="radial_face_nodes",
-    )(returned, returned, returned, from_prev, from_next, image)
+    )(odd, returned, returned, returned, near, far, image)
 
 
 def body(velocity, concentration, stiffness, block_ids, radial_weight):

time: 167 us -> 163 us (0.976)
  starting transfers between devices: 30.9 us -> 29.2 us
    ppermute x2, starting transfers between devices: 19 us -> 17.3 us  [the longest x1 17.2 us: assemble(): lax.ppermute(both, 'elem', [(e, (e + 1 ^ 1) - 1) for e in range(1, count...]
where the time goes in v3:
time: 163 us
  blocking collectives  55.2 us (34%)
  waiting for transfers between devices  33.4 us (20%)
  starting transfers between devices  29.2 us (18%)
  Pallas kernels  21.1 us (13%)
  other arithmetic  16.8 us (10%)
  local copies, waits for them, and re-layouts  5.44 us (3%)
  matrix products  1.79 us (1%)
    all_to_all x1, blocking collectives, body(): lax.all_to_all(images, 'mode', split_axis=0, concat_axis=0, tiled=True)  55.2 us
    all_to_all x1, waiting for transfers between devices, body(): lax.all_to_all(packed.reshape(groups, rows, LANES), 'mode', split_axis=0,...  33.4 us
    ppermute x1, starting transfers between devices, assemble(): lax.ppermute(both, 'elem', [(e, (e + 1 ^ 1) - 1) for e in range(1, count...  17.2 us
    all_to_all x1, starting transfers between devices, body(): lax.all_to_all(packed.reshape(groups, rows, LANES), 'mode', split_axis=0,...  11.9 us
    pallas_call x1, Pallas kernels, azimuth(): pl.pallas_call(azimuth_kernel, in_specs=[vmem, hbm, hbm, hbm, hbm, vmem],...  11.6 us
    convert_element_type x1, other arithmetic, azimuth_tables(): jnp.cos(angle).astype(jnp.bfloat16).reshape(shape)  9.05 us
    pallas_call x1, Pallas kernels, assemble(): pl.pallas_call(interior_kernel, grid=(7,), in_specs=[pl.BlockSpec(block,...  4.64 us
    optimization_barrier x1, local copies, waits for them, and re-layouts, azimuth_tables(): base = lax.optimization_barrier(base)  3.94 us
  transfers between devices with their start and end apart: 3, of which 1 were waited for; matrix products, arithmetic and copies ran while one was open for 14% of the time, Pallas kernels for 3%

profile of v3, /device:TPU:1, one launch (start us, length us, event | category | flops | bytes accessed | tf_op | source)
XLA Modules:
  0.0 163.1 jit_solution(8478725650006129686)
XLA Ops:
  0.0 0.0 copy-start
  0.0 3.1 %pack_by_element_group.1 = bf16[16,81,8,128]{3,2,1,0:T(8,128)(2,1)} custom-call(bf16[2,2,81,32,128]{4,3,2,1,0:T(8,128)(2,1)} %bitcast.49), custom_call_target="tpu_custom_call" | custom-call | tf_op jit(solution)/shard_map/pack_by_element_group/pallas_call | solution.py:80
  3.1 0.0 copy-start.5
  3.1 0.0 copy-start.4
  3.2 11.9 %all-to-all-start = ((bf16[16,648,128]{2,1,0:T(8,128)(2,1)}), bf16[16,648,128]{2,1,0:T(8,128)(2,1)S(1)}, u32[]{:S(2)}, u32[]{:S(2)}) async-start(bf16[16,648,128]{2,1,0:T(8,128)(2,1)} %bitcast.48), calls=%async_computation | async-start | bytes 5308416 | tf_op jit(solution)/shard_map/all_to_all | solution.py:310
  15.1 0.0 copy-done.5
  15.1 0.1 broadcast_compare_fusion.3
  15.2 0.1 eq.117
  15.3 0.1 eq.110
  15.4 0.1 eq.119
  15.5 0.1 eq.121
  15.6 0.0 copy-done.4
  15.6 0.1 constant_dynamic-slice_fusion
  15.7 0.2 reshape.227.weight_ref
  15.9 9.0 %cosine_convert_fusion = (bf16[16,1,32,1024]{3,2,1,0:T(8,128)(2,1)S(1)}, bf16[16,1,32,1024]{3,2,1,0:T(8,128)(2,1)S(1)}) fusion(s32[16,32]{1,0:T(8,128)S(1)} %multiply_add_fusion), kind=kLoop, calls=%fused_computation.10 | loop fusion | flops 8912896 | bytes 2099200 | tf_op jit(solution)/shard_map/convert_element_type | solution.py:37
  24.9 1.5 pad_maximum_fusion
  26.5 3.9 %copy.9 = bf16[1024,1024]{0,1:T(8,128)(2,1)} copy(bf16[1024,1024]{1,0:T(8,128)(2,1)} %bitcast.46) | data formatting | bytes 4194304 | tf_op jit(solution)/shard_map/optimization_barrier | solution.py:42
  30.4 0.0 copy-start.3
  30.4 0.0 copy-done
  30.4 0.3 convolution_bitcast_fusion
  30.8 1.5 compare_select_fusion.couple_hbm
  32.2 0.0 copy-done.3
  32.2 0.0 copy-start.2
  32.2 3.0 %power_bitcast_fusion.visc_hbm = f32[648,1024]{1,0:T(8,128)} fusion(bf16[1024,81,8]{0,2,1:T(8,128)(2,1)S(1)} %copy-done.3), kind=kLoop, calls=%fused_computation.3 | loop fusion | flops 1990656 | bytes 3981312 | tf_op jit(solution)/shard_map/pow | solution.py:315
  35.2 0.0 copy-done.2
  35.2 0.0 copy-start.1
  35.2 1.5 multiply_bitcast_fusion.fwd_hbm
  36.8 0.8 copy-done.1
  37.6 1.5 broadcast_multiply_fusion.inv_hbm
  39.1 33.4 %all-to-all-done.x_ref = bf16[16,648,128]{2,1,0:T(8,128)(2,1)S(1)} async-done(((bf16[16,648,128]{2,1,0:T(8,128)(2,1)}), bf16[16,648,128]{2,1,0:T(8,128)(2,1)S(1)}, u32[]{:S(2)}, u32[]{:S(2)}) %all-to-all-start) | async-done | bytes 2654240 | tf_op jit(solution)/shard_map/all_to_all | solution.py:310
  72.5 11.6 %azimuth_product_and_coupling.1 = bf16[16,592,128]{2,1,0:T(8,128)(2,1)S(1)} custom-call(bf16[16,648,128]{2,1,0:T(8,128)(2,1)S(1)} %all-to-all-done.x_ref, bf16[1024,1024]{1,0:T(8,128)(2,1)} %broadcast_multiply_fusion.inv_hbm, f32[648,1024]{1,0:T(8,128)} %power_bitcast_fusion.visc_hbm, bf16[1024,1024]{1,0:T(8,128)(2,1)} %multiply_bitcast_fusion.fwd_hbm, ...), custom_call_target="tpu_custom_call" | custom-call | tf_op jit(solution)/shard_map/azimuth_product_and_coupling/pallas_call | solution.py:181
  84.1 55.2 %all_to_all.10.z_ref.extra_ref.inner_ref.outer_ref = bf16[16,592,128]{2,1,0:T(8,128)(2,1)S(1)} all-to-all(bf16[16,592,128]{2,1,0:T(8,128)(2,1)S(1)} %azimuth_product_and_coupling.1), channel_id=1, replica_groups=mesh['mode'=16,'elem'=16] {'mode'}, dimensions={0} | all-to-all | bytes 4849664 | tf_op jit(solution)/shard_map/all_to_all | solution.py:337
  139.4 17.2 %collective-permute-start.1 = (bf16[2,2,80,128]{3,2,1,0:T(8,128)(2,1)S(1)}, bf16[2,2,80,128]{3,2,1,0:T(8,128)(2,1)S(1)}, u32[]{:S(2)}, u32[]{:S(2)}) collective-permute-start(bf16[2,2,80,128]{3,2,1,0:T(8,128)(2,1)S(1)} %pad_maximum_fusion.1), channel_id=1, source_target_pairs={{1,2},{2,1},{3,4},{4,3},{5,6},{6,5},{7,8},{8,7},{9,10},{10,9},{11,... | collective-permute-start | bytes 245768 | tf_op jit(solution)/shard_map/ppermute | solution.py:265
  156.6 0.1 collective-permute-start
  156.7 4.6 %interior_nodes.1.kept_ref = f32[2,2,81,32,128]{4,3,2,1,0:T(8,128)} custom-call(bf16[16,592,128]{2,1,0:T(8,128)(2,1)S(1)} %all_to_all.10.z_ref.extra_ref.inner_ref.outer_ref, bf16[16,592,128]{2,1,0:T(8,128)(2,1)S(1)} %all_to_all.10.z_ref.extra_ref.inner_ref.outer_ref), custom_call_target="tpu_custom_call" | custom-call | tf_op jit(solution)/shard_map/interior_nodes/pallas_call | solution.py:273
  161.3 0.0 collective-permute-done.1.far_ref
  161.3 0.0 collective-permute-done.near_ref
  161.3 1.7 %radial_face_nodes.1 = f32[2,2,81,32,128]{4,3,2,1,0:T(8,128)} custom-call(s32[1]{0:T(128)} %bitcast.odd_ref, bf16[16,592,128]{2,1,0:T(8,128)(2,1)S(1)} %all_to_all.10.z_ref.extra_ref.inner_ref.outer_ref, bf16[16,592,128]{2,1,0:T(8,128)(2,1)S(1)} %all_to_all.10.z_ref.extra_ref.inner_ref.outer_ref, ...), custom_call_target="tpu_custom_call", output_to_operand_aliasing={{}: (6, {})} | custom-call | tf_op jit(solution)/shard_map/radial_face_nodes/pallas_call | solution.py:283
  (13 shorter events, 0.1 us)
Async XLA Ops:
  0.0 30.4 %copy-start = (bf16[4,81,81]{2,0,1:T(4,128)(2,1)S(1)}, bf16[4,81,81]{2,0,1:T(4,128)(2,1)}, u32[]{:S(2)}) copy-start(bf16[4,81,81]{2,0,1:T(4,128)(2,1)} %param.7) | copy-start | bytes 157468
  3.1 11.9 %copy-start.5 = (s32[128]{0:T(128)S(1)}, s32[128]{0:T(128)}, u32[]{:S(2)}) copy-start(s32[128]{0:T(128)} %param.8) | copy-start | bytes 1540
  3.1 12.5 %copy-start.4 = (f32[81,128]{1,0:T(8,128)S(1)}, f32[81,128]{1,0:T(8,128)}, u32[]{:S(2)}) copy-start(f32[81,128]{1,0:T(8,128)} %param.9) | copy-start | bytes 124420
  3.2 69.3 %all-to-all-start = ((bf16[16,648,128]{2,1,0:T(8,128)(2,1)}), bf16[16,648,128]{2,1,0:T(8,128)(2,1)S(1)}, u32[]{:S(2)}, u32[]{:S(2)}) async-start(bf16[16,648,128]{2,1,0:T(8,128)(2,1)} %bitcast.48), calls=%async_computation | async-start | bytes 5308416 | tf_op jit(solution)/shard_map/all_to_all | solution.py:310
  30.4 1.8 %copy-start.3 = (bf16[1024,81,8]{0,2,1:T(8,128)(2,1)S(1)}, bf16[1024,81,8]{0,2,1:T(8,128)(2,1)}, u32[]{:S(2)}) copy-start(bf16[1024,81,8]{0,2,1:T(8,128)(2,1)} %param.6) | copy-start | bytes 3981316
  32.2 3.0 %copy-start.2 = (bf16[1024,1024]{0,1:T(8,128)(2,1)S(1)}, bf16[1024,1024]{0,1:T(8,128)(2,1)}, u32[]{:S(2)}) copy-start(bf16[1024,1024]{0,1:T(8,128)(2,1)} %copy.9) | copy-start | bytes 6291460
  35.2 2.3 %copy-start.1 = (bf16[16,2,32,1024]{3,2,1,0:T(8,128)(2,1)S(1)}, bf16[16,2,32,1024]{3,2,1,0:T(8,128)(2,1)}, u32[]{:S(2)}) copy-start(bf16[16,2,32,1024]{3,2,1,0:T(8,128)(2,1)} %pad_maximum_fusion) | copy-start | bytes 6291460
  139.4 22.0 %collective-permute-start.1 = (bf16[2,2,80,128]{3,2,1,0:T(8,128)(2,1)S(1)}, bf16[2,2,80,128]{3,2,1,0:T(8,128)(2,1)S(1)}, u32[]{:S(2)}, u32[]{:S(2)}) collective-permute-start(bf16[2,2,80,128]{3,2,1,0:T(8,128)(2,1)S(1)} %pad_maximum_fusion.1), channel_id=1, source_target_pairs={{1,2},{2,1},{3,4},{4,3},{5,6},{6,5},{7,8},{8,7},{9,10},{10,9},{11,... | collective-permute-start | bytes 245768 | tf_op jit(solution)/shard_map/ppermute | solution.py:265
  156.6 4.8 %collective-permute-start = (bf16[2,2,80,128]{3,2,1,0:T(8,128)(2,1)S(1)}, bf16[2,2,80,128]{3,2,1,0:T(8,128)(2,1)S(1)}, u32[]{:S(2)}, u32[]{:S(2)}) collective-permute-start(bf16[2,2,80,128]{3,2,1,0:T(8,128)(2,1)S(1)} %pad_maximum_fusion.1), channel_id=1, source_target_pairs={{0,1},{1,0},{2,3},{3,2},{4,5},{5,4},{6,7},{7,6},{8,9},{9,8},{10,11... | collective-permute-start | bytes 245768 | tf_op jit(solution)/shard_map/ppermute | solution.py:264

commit v4 on v3

--- a/solution.py
+++ b/solution.py
@@ -14,7 +14,7 @@
 LANES = 128
 FACE = 9
 EXTRA = 16
-STAGES = (3, 5, 7)
+PLANES = 256
 
 packing_limit = 0.68
 krieger_power = 1.82
@@ -102,43 +102,61 @@
 
 
 def azimuth_kernel(x_ref, inv_hbm, visc_hbm, fwd_hbm, couple_hbm, weight_ref, o_ref,
-                   inv_ref, visc_ref, fwd_ref, couple_ref, field_ref, image_ref, sems):
+                   inv_ref, visc_ref, fwd_ref, couple_ref, field_ref, product_ref, image_ref,
+                   sems):
     groups, rows, _ = x_ref.shape
-    pairs = (
-        (inv_hbm, inv_ref), (visc_hbm, visc_ref), (fwd_hbm, fwd_ref), (couple_hbm, couple_ref),
-    )
-    copies = [
-        pltpu.make_async_copy(source, target, sems.at[k])
-        for k, (source, target) in enumerate(pairs)
+    parts = NPHI // PLANES
+    planes = [slice(q * PLANES, (q + 1) * PLANES) for q in range(parts)]
+
+    def copy_of(source, target, place):
+        return pltpu.make_async_copy(source, target, sems.at[place])
+
+    tables = [
+        (
+            copy_of(inv_hbm.at[:, planes[q]], inv_ref.at[:, planes[q]], 2 * q),
+            copy_of(visc_hbm.at[:, planes[q]], visc_ref.at[:, planes[q]], 2 * q + 1),
+        )
+        for q in range(parts)
     ]
-    copies[0].start()
+    forward = copy_of(fwd_hbm, fwd_ref, 2 * parts)
+    coupling = copy_of(couple_hbm, couple_ref, 2 * parts + 1)
+    for part in tables:
+        for copy in part:
+            copy.start()
+    forward.start()
+    coupling.start()
     lane = lax.broadcasted_iota(jnp.int32, (rows, LANES), 1)
     low = lane < LANES // 2
-    for t in range(groups // 2):
-        first, second = swap_halves(
-            x_ref[2 * t].astype(jnp.float32), x_ref[2 * t + 1].astype(jnp.float32), low
-        )
-        field_ref[0, :, t * LANES:(t + 1) * LANES] = first.astype(jnp.bfloat16)
-        field_ref[1, :, t * LANES:(t + 1) * LANES] = second.astype(jnp.bfloat16)
-        if t in STAGES:
-            copies[STAGES.index(t) + 1].start()
+
+    def gather_field(c):
+        for t in range(groups // 2):
+            pair = swap_halves(
+                x_ref[2 * t].astype(jnp.float32), x_ref[2 * t + 1].astype(jnp.float32), low
+            )
+            field_ref[c, :, t * LANES:(t + 1) * LANES] = pair[c].astype(jnp.bfloat16)
+
+    gather_field(0)
+    for q in range(parts):
+        for copy in tables[q]:
+            copy.wait()
+        for c in range(2):
+            if q == 0 and c == 1:
+                gather_field(1)
+            physical = jnp.dot(
+                field_ref[c], inv_ref[:, planes[q]], preferred_element_type=jnp.float32
+            )
+            product_ref[c, :, planes[q]] = (visc_ref[:, planes[q]] * physical).astype(
+                jnp.bfloat16
+            )
+    forward.wait()
+    coupling.wait()
+    column = lax.broadcasted_iota(jnp.int32, (1, 2 * MODES), 1)
+    order = (column // 64) * 32 + column % 32
+    scale = 4.0 * (order.astype(jnp.float32) / MODES) ** 2
     for c in range(2):
-        if c == 0:
-            copies[0].wait()
-        physical = jnp.dot(field_ref[c], inv_ref[...], preferred_element_type=jnp.float32)
-        if c == 0:
-            copies[1].wait()
-        product = (visc_ref[...] * physical).astype(jnp.bfloat16)
-        if c == 0:
-            copies[2].wait()
         spectral = jnp.dot(
-            product, fwd_ref[...], preferred_element_type=jnp.float32
+            product_ref[c], fwd_ref[...], preferred_element_type=jnp.float32
         ).astype(jnp.bfloat16)
-        column = lax.broadcasted_iota(jnp.int32, (1, 2 * MODES), 1)
-        order = (column // 64) * 32 + column % 32
-        scale = 4.0 * (order.astype(jnp.float32) / MODES) ** 2
-        if c == 0:
-            copies[3].wait()
         image_ref[c] = jnp.dot(
             couple_ref[...], spectral, preferred_element_type=jnp.float32
         ) + (weight_ref[...] * scale) * spectral.astype(jnp.float32)
@@ -185,8 +203,9 @@
         out_shape=jax.ShapeDtypeStruct((groups, sent, LANES), jnp.bfloat16),
         scratch_shapes=[pltpu.VMEM(value.shape, value.dtype) for value in held] + [
             pltpu.VMEM((2, rows, 2 * MODES), jnp.bfloat16),
+            pltpu.VMEM((2, rows, NPHI), jnp.bfloat16),
             pltpu.VMEM((2, rows, 2 * MODES), jnp.float32),
-            pltpu.SemaphoreType.DMA((len(held),)),
+            pltpu.SemaphoreType.DMA((2 * (NPHI // PLANES) + 2,)),
         ],
         compiler_params=params(40),
         name="azimuth_product_and_coupling",

time: 163 us -> 162 us (level)
  no operation moved by 1% of the time
where the time goes in v4:
time: 162 us
  blocking collectives  55.2 us (34%)
  waiting for transfers between devices  33.4 us (21%)
  starting transfers between devices  29.2 us (18%)
  Pallas kernels  19.9 us (12%)
  other arithmetic  16.8 us (10%)
  local copies, waits for them, and re-layouts  5.44 us (3%)
  matrix products  1.79 us (1%)
    all_to_all x1, blocking collectives, body(): lax.all_to_all(images, 'mode', split_axis=0, concat_axis=0, tiled=True)  55.2 us
    all_to_all x1, waiting for transfers between devices, body(): lax.all_to_all(packed.reshape(groups, rows, LANES), 'mode', split_axis=0,...  33.4 us
    ppermute x1, starting transfers between devices, assemble(): lax.ppermute(both, 'elem', [(e, (e + 1 ^ 1) - 1) for e in range(1, count...  17.2 us
    all_to_all x1, starting transfers between devices, body(): lax.all_to_all(packed.reshape(groups, rows, LANES), 'mode', split_axis=0,...  11.9 us
    pallas_call x1, Pallas kernels, azimuth(): pl.pallas_call(azimuth_kernel, in_specs=[vmem, hbm, hbm, hbm, hbm, vmem],...  10.5 us
    convert_element_type x1, other arithmetic, azimuth_tables(): jnp.cos(angle).astype(jnp.bfloat16).reshape(shape)  9.05 us
    pallas_call x1, Pallas kernels, assemble(): pl.pallas_call(interior_kernel, grid=(7,), in_specs=[pl.BlockSpec(block,...  4.64 us
    optimization_barrier x1, local copies, waits for them, and re-layouts, azimuth_tables(): base = lax.optimization_barrier(base)  3.94 us
  transfers between devices with their start and end apart: 3, of which 1 were waited for; matrix products, arithmetic and copies ran while one was open for 14% of the time, Pallas kernels for 3%

profile of v4, /device:TPU:1, one launch (start us, length us, event | category | flops | bytes accessed | tf_op | source)
XLA Modules:
  0.0 161.9 jit_solution(1131498012688494774)
XLA Ops:
  0.0 0.0 copy-start
  0.0 3.1 %pack_by_element_group.1 = bf16[16,81,8,128]{3,2,1,0:T(8,128)(2,1)} custom-call(bf16[2,2,81,32,128]{4,3,2,1,0:T(8,128)(2,1)} %bitcast.49), custom_call_target="tpu_custom_call" | custom-call | tf_op jit(solution)/shard_map/pack_by_element_group/pallas_call | solution.py:80
  3.1 0.0 copy-start.5
  3.1 0.0 copy-start.4
  3.2 11.9 %all-to-all-start = ((bf16[16,648,128]{2,1,0:T(8,128)(2,1)}), bf16[16,648,128]{2,1,0:T(8,128)(2,1)S(1)}, u32[]{:S(2)}, u32[]{:S(2)}) async-start(bf16[16,648,128]{2,1,0:T(8,128)(2,1)} %bitcast.48), calls=%async_computation | async-start | bytes 5308416 | tf_op jit(solution)/shard_map/all_to_all | solution.py:329
  15.1 0.0 copy-done.5
  15.1 0.1 broadcast_compare_fusion.3
  15.2 0.1 eq.117
  15.3 0.1 eq.110
  15.4 0.1 eq.119
  15.5 0.1 eq.121
  15.6 0.0 copy-done.4
  15.6 0.1 constant_dynamic-slice_fusion
  15.7 0.2 reshape.227.weight_ref
  15.9 9.0 %cosine_convert_fusion = (bf16[16,1,32,1024]{3,2,1,0:T(8,128)(2,1)S(1)}, bf16[16,1,32,1024]{3,2,1,0:T(8,128)(2,1)S(1)}) fusion(s32[16,32]{1,0:T(8,128)S(1)} %multiply_add_fusion), kind=kLoop, calls=%fused_computation.10 | loop fusion | flops 8912896 | bytes 2099200 | tf_op jit(solution)/shard_map/convert_element_type | solution.py:37
  24.9 1.5 pad_maximum_fusion
  26.5 3.9 %copy.9 = bf16[1024,1024]{0,1:T(8,128)(2,1)} copy(bf16[1024,1024]{1,0:T(8,128)(2,1)} %bitcast.46) | data formatting | bytes 4194304 | tf_op jit(solution)/shard_map/optimization_barrier | solution.py:42
  30.4 0.0 copy-start.3
  30.4 0.0 copy-done
  30.4 0.3 convolution_bitcast_fusion
  30.8 1.5 compare_select_fusion.couple_hbm
  32.2 0.0 copy-done.3
  32.2 0.0 copy-start.2
  32.2 3.0 %power_bitcast_fusion.visc_hbm = f32[648,1024]{1,0:T(8,128)} fusion(bf16[1024,81,8]{0,2,1:T(8,128)(2,1)S(1)} %copy-done.3), kind=kLoop, calls=%fused_computation.3 | loop fusion | flops 1990656 | bytes 3981312 | tf_op jit(solution)/shard_map/pow | solution.py:334
  35.2 0.0 copy-done.2
  35.2 0.0 copy-start.1
  35.2 1.5 multiply_bitcast_fusion.fwd_hbm
  36.8 0.8 copy-done.1
  37.6 1.5 broadcast_multiply_fusion.inv_hbm
  39.1 33.4 %all-to-all-done.x_ref = bf16[16,648,128]{2,1,0:T(8,128)(2,1)S(1)} async-done(((bf16[16,648,128]{2,1,0:T(8,128)(2,1)}), bf16[16,648,128]{2,1,0:T(8,128)(2,1)S(1)}, u32[]{:S(2)}, u32[]{:S(2)}) %all-to-all-start) | async-done | bytes 2654240 | tf_op jit(solution)/shard_map/all_to_all | solution.py:329
  72.5 10.5 %azimuth_product_and_coupling.1 = bf16[16,592,128]{2,1,0:T(8,128)(2,1)S(1)} custom-call(bf16[16,648,128]{2,1,0:T(8,128)(2,1)S(1)} %all-to-all-done.x_ref, bf16[1024,1024]{1,0:T(8,128)(2,1)} %broadcast_multiply_fusion.inv_hbm, f32[648,1024]{1,0:T(8,128)} %power_bitcast_fusion.visc_hbm, bf16[1024,1024]{1,0:T(8,128)(2,1)} %multiply_bitcast_fusion.fwd_hbm, ...), custom_call_target="tpu_custom_call" | custom-call | tf_op jit(solution)/shard_map/azimuth_product_and_coupling/pallas_call | solution.py:199
  82.9 55.2 %all_to_all.10.z_ref.extra_ref.inner_ref.outer_ref = bf16[16,592,128]{2,1,0:T(8,128)(2,1)S(1)} all-to-all(bf16[16,592,128]{2,1,0:T(8,128)(2,1)S(1)} %azimuth_product_and_coupling.1), channel_id=1, replica_groups=mesh['mode'=16,'elem'=16] {'mode'}, dimensions={0} | all-to-all | bytes 4849664 | tf_op jit(solution)/shard_map/all_to_all | solution.py:356
  138.2 17.2 %collective-permute-start.1 = (bf16[2,2,80,128]{3,2,1,0:T(8,128)(2,1)S(1)}, bf16[2,2,80,128]{3,2,1,0:T(8,128)(2,1)S(1)}, u32[]{:S(2)}, u32[]{:S(2)}) collective-permute-start(bf16[2,2,80,128]{3,2,1,0:T(8,128)(2,1)S(1)} %pad_maximum_fusion.1), channel_id=1, source_target_pairs={{1,2},{2,1},{3,4},{4,3},{5,6},{6,5},{7,8},{8,7},{9,10},{10,9},{11,... | collective-permute-start | bytes 245768 | tf_op jit(solution)/shard_map/ppermute | solution.py:284
  155.4 0.1 collective-permute-start
  155.5 4.6 %interior_nodes.1.kept_ref = f32[2,2,81,32,128]{4,3,2,1,0:T(8,128)} custom-call(bf16[16,592,128]{2,1,0:T(8,128)(2,1)S(1)} %all_to_all.10.z_ref.extra_ref.inner_ref.outer_ref, bf16[16,592,128]{2,1,0:T(8,128)(2,1)S(1)} %all_to_all.10.z_ref.extra_ref.inner_ref.outer_ref), custom_call_target="tpu_custom_call" | custom-call | tf_op jit(solution)/shard_map/interior_nodes/pallas_call | solution.py:292
  160.2 0.0 collective-permute-done.1.far_ref
  160.2 0.0 collective-permute-done.near_ref
  160.2 1.7 %radial_face_nodes.1 = f32[2,2,81,32,128]{4,3,2,1,0:T(8,128)} custom-call(s32[1]{0:T(128)} %bitcast.odd_ref, bf16[16,592,128]{2,1,0:T(8,128)(2,1)S(1)} %all_to_all.10.z_ref.extra_ref.inner_ref.outer_ref, bf16[16,592,128]{2,1,0:T(8,128)(2,1)S(1)} %all_to_all.10.z_ref.extra_ref.inner_ref.outer_ref, ...), custom_call_target="tpu_custom_call", output_to_operand_aliasing={{}: (6, {})} | custom-call | tf_op jit(solution)/shard_map/radial_face_nodes/pallas_call | solution.py:302
  (13 shorter events, 0.1 us)
Async XLA Ops:
  0.0 30.4 %copy-start = (bf16[4,81,81]{2,0,1:T(4,128)(2,1)S(1)}, bf16[4,81,81]{2,0,1:T(4,128)(2,1)}, u32[]{:S(2)}) copy-start(bf16[4,81,81]{2,0,1:T(4,128)(2,1)} %param.7) | copy-start | bytes 157468
  3.1 11.9 %copy-start.5 = (s32[128]{0:T(128)S(1)}, s32[128]{0:T(128)}, u32[]{:S(2)}) copy-start(s32[128]{0:T(128)} %param.8) | copy-start | bytes 1540
  3.1 12.5 %copy-start.4 = (f32[81,128]{1,0:T(8,128)S(1)}, f32[81,128]{1,0:T(8,128)}, u32[]{:S(2)}) copy-start(f32[81,128]{1,0:T(8,128)} %param.9) | copy-start | bytes 124420
  3.2 69.3 %all-to-all-start = ((bf16[16,648,128]{2,1,0:T(8,128)(2,1)}), bf16[16,648,128]{2,1,0:T(8,128)(2,1)S(1)}, u32[]{:S(2)}, u32[]{:S(2)}) async-start(bf16[16,648,128]{2,1,0:T(8,128)(2,1)} %bitcast.48), calls=%async_computation | async-start | bytes 5308416 | tf_op jit(solution)/shard_map/all_to_all | solution.py:329
  30.4 1.8 %copy-start.3 = (bf16[1024,81,8]{0,2,1:T(8,128)(2,1)S(1)}, bf16[1024,81,8]{0,2,1:T(8,128)(2,1)}, u32[]{:S(2)}) copy-start(bf16[1024,81,8]{0,2,1:T(8,128)(2,1)} %param.6) | copy-start | bytes 3981316
  32.2 3.0 %copy-start.2 = (bf16[1024,1024]{0,1:T(8,128)(2,1)S(1)}, bf16[1024,1024]{0,1:T(8,128)(2,1)}, u32[]{:S(2)}) copy-start(bf16[1024,1024]{0,1:T(8,128)(2,1)} %copy.9) | copy-start | bytes 6291460
  35.2 2.3 %copy-start.1 = (bf16[16,2,32,1024]{3,2,1,0:T(8,128)(2,1)S(1)}, bf16[16,2,32,1024]{3,2,1,0:T(8,128)(2,1)}, u32[]{:S(2)}) copy-start(bf16[16,2,32,1024]{3,2,1,0:T(8,128)(2,1)} %pad_maximum_fusion) | copy-start | bytes 6291460
  138.2 22.0 %collective-permute-start.1 = (bf16[2,2,80,128]{3,2,1,0:T(8,128)(2,1)S(1)}, bf16[2,2,80,128]{3,2,1,0:T(8,128)(2,1)S(1)}, u32[]{:S(2)}, u32[]{:S(2)}) collective-permute-start(bf16[2,2,80,128]{3,2,1,0:T(8,128)(2,1)S(1)} %pad_maximum_fusion.1), channel_id=1, source_target_pairs={{1,2},{2,1},{3,4},{4,3},{5,6},{6,5},{7,8},{8,7},{9,10},{10,9},{11,... | collective-permute-start | bytes 245768 | tf_op jit(solution)/shard_map/ppermute | solution.py:284
  155.4 4.8 %collective-permute-start = (bf16[2,2,80,128]{3,2,1,0:T(8,128)(2,1)S(1)}, bf16[2,2,80,128]{3,2,1,0:T(8,128)(2,1)S(1)}, u32[]{:S(2)}, u32[]{:S(2)}) collective-permute-start(bf16[2,2,80,128]{3,2,1,0:T(8,128)(2,1)S(1)} %pad_maximum_fusion.1), channel_id=1, source_target_pairs={{0,1},{1,0},{2,3},{3,2},{4,5},{5,4},{6,7},{7,6},{8,9},{9,8},{10,11... | collective-permute-start | bytes 245768 | tf_op jit(solution)/shard_map/ppermute | solution.py:283

commit v5 on v4

--- a/solution.py
+++ b/solution.py
@@ -102,8 +102,7 @@
 
 
 def azimuth_kernel(x_ref, inv_hbm, visc_hbm, fwd_hbm, couple_hbm, weight_ref, o_ref,
-                   inv_ref, visc_ref, fwd_ref, couple_ref, field_ref, product_ref, image_ref,
-                   sems):
+                   inv_ref, visc_ref, fwd_ref, couple_ref, field_ref, product_ref, sems):
     groups, rows, _ = x_ref.shape
     parts = NPHI // PLANES
     planes = [slice(q * PLANES, (q + 1) * PLANES) for q in range(parts)]
@@ -154,20 +153,27 @@
     order = (column // 64) * 32 + column % 32
     scale = 4.0 * (order.astype(jnp.float32) / MODES) ** 2
     for c in range(2):
-        spectral = jnp.dot(
+        field_ref[c] = jnp.dot(
             product_ref[c], fwd_ref[...], preferred_element_type=jnp.float32
         ).astype(jnp.bfloat16)
-        image_ref[c] = jnp.dot(
-            couple_ref[...], spectral, preferred_element_type=jnp.float32
-        ) + (weight_ref[...] * scale) * spectral.astype(jnp.float32)
-    for t in range(groups // 2):
-        pair = swap_halves(
-            image_ref[0, :, t * LANES:(t + 1) * LANES],
-            image_ref[1, :, t * LANES:(t + 1) * LANES],
-            low,
-        )
-        for half in range(2):
-            merge_axial(o_ref.at[2 * t + half], pair[half], rows // NODE)
+    wide = 2 * LANES
+    for n in range(2 * MODES // wide):
+        columns = slice(n * wide, (n + 1) * wide)
+        images = []
+        for c in range(2):
+            spectral = field_ref[c, :, columns]
+            images.append(
+                jnp.dot(couple_ref[...], spectral, preferred_element_type=jnp.float32)
+                + (weight_ref[...] * scale[:, columns]) * spectral.astype(jnp.float32)
+            )
+        for t in range(2):
+            pair = swap_halves(
+                images[0][:, t * LANES:(t + 1) * LANES],
+                images[1][:, t * LANES:(t + 1) * LANES],
+                low,
+            )
+            for half in range(2):
+                merge_axial(o_ref.at[4 * n + 2 * t + half], pair[half], rows // NODE)
 
 
 def merge_axial(o_ref, image, piece):
@@ -204,7 +210,6 @@
         scratch_shapes=[pltpu.VMEM(value.shape, value.dtype) for value in held] + [
             pltpu.VMEM((2, rows, 2 * MODES), jnp.bfloat16),
             pltpu.VMEM((2, rows, NPHI), jnp.bfloat16),
-            pltpu.VMEM((2, rows, 2 * MODES), jnp.float32),
             pltpu.SemaphoreType.DMA((2 * (NPHI // PLANES) + 2,)),
         ],
         compiler_params=params(40),

time: 162 us -> 162 us (level)
  no operation moved by 1% of the time
where the time goes in v5:
time: 162 us
  blocking collectives  55.2 us (34%)
  waiting for transfers between devices  33.4 us (21%)
  starting transfers between devices  29.2 us (18%)
  Pallas kernels  19.9 us (12%)
  other arithmetic  16.8 us (10%)
  local copies, waits for them, and re-layouts  5.44 us (3%)
  matrix products  1.79 us (1%)
    all_to_all x1, blocking collectives, body(): lax.all_to_all(images, 'mode', split_axis=0, concat_axis=0, tiled=True)  55.2 us
    all_to_all x1, waiting for transfers between devices, body(): lax.all_to_all(packed.reshape(groups, rows, LANES), 'mode', split_axis=0,...  33.4 us
    ppermute x1, starting transfers between devices, assemble(): lax.ppermute(both, 'elem', [(e, (e + 1 ^ 1) - 1) for e in range(1, count...  17.2 us
    all_to_all x1, starting transfers between devices, body(): lax.all_to_all(packed.reshape(groups, rows, LANES), 'mode', split_axis=0,...  11.9 us
    pallas_call x1, Pallas kernels, azimuth(): pl.pallas_call(azimuth_kernel, in_specs=[vmem, hbm, hbm, hbm, hbm, vmem],...  10.4 us
    convert_element_type x1, other arithmetic, azimuth_tables(): jnp.cos(angle).astype(jnp.bfloat16).reshape(shape)  9.05 us
    pallas_call x1, Pallas kernels, assemble(): pl.pallas_call(interior_kernel, grid=(7,), in_specs=[pl.BlockSpec(block,...  4.64 us
    optimization_barrier x1, local copies, waits for them, and re-layouts, azimuth_tables(): base = lax.optimization_barrier(base)  3.94 us
  transfers between devices with their start and end apart: 3, of which 1 were waited for; matrix products, arithmetic and copies ran while one was open for 14% of the time, Pallas kernels for 3%

profile of v5, /device:TPU:1, one launch (start us, length us, event | category | flops | bytes accessed | tf_op | source)
XLA Modules:
  0.0 161.8 jit_solution(12090619508587266581)
XLA Ops:
  0.0 0.0 copy-start
  0.0 3.1 %pack_by_element_group.1 = bf16[16,81,8,128]{3,2,1,0:T(8,128)(2,1)} custom-call(bf16[2,2,81,32,128]{4,3,2,1,0:T(8,128)(2,1)} %bitcast.49), custom_call_target="tpu_custom_call" | custom-call | tf_op jit(solution)/shard_map/pack_by_element_group/pallas_call | solution.py:80
  3.1 0.0 copy-start.5
  3.1 0.0 copy-start.4
  3.2 11.9 %all-to-all-start = ((bf16[16,648,128]{2,1,0:T(8,128)(2,1)}), bf16[16,648,128]{2,1,0:T(8,128)(2,1)S(1)}, u32[]{:S(2)}, u32[]{:S(2)}) async-start(bf16[16,648,128]{2,1,0:T(8,128)(2,1)} %bitcast.48), calls=%async_computation | async-start | bytes 5308416 | tf_op jit(solution)/shard_map/all_to_all | solution.py:334
  15.1 0.0 copy-done.5
  15.1 0.1 broadcast_compare_fusion.3
  15.2 0.1 eq.117
  15.3 0.1 eq.110
  15.4 0.1 eq.119
  15.5 0.1 eq.121
  15.6 0.0 copy-done.4
  15.6 0.1 constant_dynamic-slice_fusion
  15.7 0.2 reshape.227.weight_ref
  15.9 9.0 %cosine_convert_fusion = (bf16[16,1,32,1024]{3,2,1,0:T(8,128)(2,1)S(1)}, bf16[16,1,32,1024]{3,2,1,0:T(8,128)(2,1)S(1)}) fusion(s32[16,32]{1,0:T(8,128)S(1)} %multiply_add_fusion), kind=kLoop, calls=%fused_computation.10 | loop fusion | flops 8912896 | bytes 2099200 | tf_op jit(solution)/shard_map/convert_element_type | solution.py:37
  24.9 1.5 pad_maximum_fusion
  26.5 3.9 %copy.9 = bf16[1024,1024]{0,1:T(8,128)(2,1)} copy(bf16[1024,1024]{1,0:T(8,128)(2,1)} %bitcast.46) | data formatting | bytes 4194304 | tf_op jit(solution)/shard_map/optimization_barrier | solution.py:42
  30.4 0.0 copy-start.3
  30.4 0.0 copy-done
  30.4 0.3 convolution_bitcast_fusion
  30.8 1.5 compare_select_fusion.couple_hbm
  32.2 0.0 copy-done.3
  32.2 0.0 copy-start.2
  32.2 3.0 %power_bitcast_fusion.visc_hbm = f32[648,1024]{1,0:T(8,128)} fusion(bf16[1024,81,8]{0,2,1:T(8,128)(2,1)S(1)} %copy-done.3), kind=kLoop, calls=%fused_computation.3 | loop fusion | flops 1990656 | bytes 3981312 | tf_op jit(solution)/shard_map/pow | solution.py:339
  35.2 0.0 copy-done.2
  35.2 0.0 copy-start.1
  35.2 1.5 multiply_bitcast_fusion.fwd_hbm
  36.8 0.8 copy-done.1
  37.6 1.5 broadcast_multiply_fusion.inv_hbm
  39.1 33.4 %all-to-all-done.x_ref = bf16[16,648,128]{2,1,0:T(8,128)(2,1)S(1)} async-done(((bf16[16,648,128]{2,1,0:T(8,128)(2,1)}), bf16[16,648,128]{2,1,0:T(8,128)(2,1)S(1)}, u32[]{:S(2)}, u32[]{:S(2)}) %all-to-all-start) | async-done | bytes 2654240 | tf_op jit(solution)/shard_map/all_to_all | solution.py:334
  72.5 10.4 %azimuth_product_and_coupling.1 = bf16[16,592,128]{2,1,0:T(8,128)(2,1)S(1)} custom-call(bf16[16,648,128]{2,1,0:T(8,128)(2,1)S(1)} %all-to-all-done.x_ref, bf16[1024,1024]{1,0:T(8,128)(2,1)} %broadcast_multiply_fusion.inv_hbm, f32[648,1024]{1,0:T(8,128)} %power_bitcast_fusion.visc_hbm, bf16[1024,1024]{1,0:T(8,128)(2,1)} %multiply_bitcast_fusion.fwd_hbm, ...), custom_call_target="tpu_custom_call" | custom-call | tf_op jit(solution)/shard_map/azimuth_product_and_coupling/pallas_call | solution.py:205
  82.9 55.2 %all_to_all.10.z_ref.extra_ref.inner_ref.outer_ref = bf16[16,592,128]{2,1,0:T(8,128)(2,1)S(1)} all-to-all(bf16[16,592,128]{2,1,0:T(8,128)(2,1)S(1)} %azimuth_product_and_coupling.1), channel_id=1, replica_groups=mesh['mode'=16,'elem'=16] {'mode'}, dimensions={0} | all-to-all | bytes 4849664 | tf_op jit(solution)/shard_map/all_to_all | solution.py:361
  138.1 17.2 %collective-permute-start.1 = (bf16[2,2,80,128]{3,2,1,0:T(8,128)(2,1)S(1)}, bf16[2,2,80,128]{3,2,1,0:T(8,128)(2,1)S(1)}, u32[]{:S(2)}, u32[]{:S(2)}) collective-permute-start(bf16[2,2,80,128]{3,2,1,0:T(8,128)(2,1)S(1)} %pad_maximum_fusion.1), channel_id=1, source_target_pairs={{1,2},{2,1},{3,4},{4,3},{5,6},{6,5},{7,8},{8,7},{9,10},{10,9},{11,... | collective-permute-start | bytes 245768 | tf_op jit(solution)/shard_map/ppermute | solution.py:289
  155.4 0.1 collective-permute-start
  155.5 4.6 %interior_nodes.1.kept_ref = f32[2,2,81,32,128]{4,3,2,1,0:T(8,128)} custom-call(bf16[16,592,128]{2,1,0:T(8,128)(2,1)S(1)} %all_to_all.10.z_ref.extra_ref.inner_ref.outer_ref, bf16[16,592,128]{2,1,0:T(8,128)(2,1)S(1)} %all_to_all.10.z_ref.extra_ref.inner_ref.outer_ref), custom_call_target="tpu_custom_call" | custom-call | tf_op jit(solution)/shard_map/interior_nodes/pallas_call | solution.py:297
  160.1 0.0 collective-permute-done.1.far_ref
  160.1 0.0 collective-permute-done.near_ref
  160.1 1.7 %radial_face_nodes.1 = f32[2,2,81,32,128]{4,3,2,1,0:T(8,128)} custom-call(s32[1]{0:T(128)} %bitcast.odd_ref, bf16[16,592,128]{2,1,0:T(8,128)(2,1)S(1)} %all_to_all.10.z_ref.extra_ref.inner_ref.outer_ref, bf16[16,592,128]{2,1,0:T(8,128)(2,1)S(1)} %all_to_all.10.z_ref.extra_ref.inner_ref.outer_ref, ...), custom_call_target="tpu_custom_call", output_to_operand_aliasing={{}: (6, {})} | custom-call | tf_op jit(solution)/shard_map/radial_face_nodes/pallas_call | solution.py:307
  (13 shorter events, 0.1 us)
Async XLA Ops:
  0.0 30.4 %copy-start = (bf16[4,81,81]{2,0,1:T(4,128)(2,1)S(1)}, bf16[4,81,81]{2,0,1:T(4,128)(2,1)}, u32[]{:S(2)}) copy-start(bf16[4,81,81]{2,0,1:T(4,128)(2,1)} %param.7) | copy-start | bytes 157468
  3.1 11.9 %copy-start.5 = (s32[128]{0:T(128)S(1)}, s32[128]{0:T(128)}, u32[]{:S(2)}) copy-start(s32[128]{0:T(128)} %param.8) | copy-start | bytes 1540
  3.1 12.5 %copy-start.4 = (f32[81,128]{1,0:T(8,128)S(1)}, f32[81,128]{1,0:T(8,128)}, u32[]{:S(2)}) copy-start(f32[81,128]{1,0:T(8,128)} %param.9) | copy-start | bytes 124420
  3.2 69.3 %all-to-all-start = ((bf16[16,648,128]{2,1,0:T(8,128)(2,1)}), bf16[16,648,128]{2,1,0:T(8,128)(2,1)S(1)}, u32[]{:S(2)}, u32[]{:S(2)}) async-start(bf16[16,648,128]{2,1,0:T(8,128)(2,1)} %bitcast.48), calls=%async_computation | async-start | bytes 5308416 | tf_op jit(solution)/shard_map/all_to_all | solution.py:334
  30.4 1.8 %copy-start.3 = (bf16[1024,81,8]{0,2,1:T(8,128)(2,1)S(1)}, bf16[1024,81,8]{0,2,1:T(8,128)(2,1)}, u32[]{:S(2)}) copy-start(bf16[1024,81,8]{0,2,1:T(8,128)(2,1)} %param.6) | copy-start | bytes 3981316
  32.2 3.0 %copy-start.2 = (bf16[1024,1024]{0,1:T(8,128)(2,1)S(1)}, bf16[1024,1024]{0,1:T(8,128)(2,1)}, u32[]{:S(2)}) copy-start(bf16[1024,1024]{0,1:T(8,128)(2,1)} %copy.9) | copy-start | bytes 6291460
  35.2 2.3 %copy-start.1 = (bf16[16,2,32,1024]{3,2,1,0:T(8,128)(2,1)S(1)}, bf16[16,2,32,1024]{3,2,1,0:T(8,128)(2,1)}, u32[]{:S(2)}) copy-start(bf16[16,2,32,1024]{3,2,1,0:T(8,128)(2,1)} %pad_maximum_fusion) | copy-start | bytes 6291460
  138.1 22.0 %collective-permute-start.1 = (bf16[2,2,80,128]{3,2,1,0:T(8,128)(2,1)S(1)}, bf16[2,2,80,128]{3,2,1,0:T(8,128)(2,1)S(1)}, u32[]{:S(2)}, u32[]{:S(2)}) collective-permute-start(bf16[2,2,80,128]{3,2,1,0:T(8,128)(2,1)S(1)} %pad_maximum_fusion.1), channel_id=1, source_target_pairs={{1,2},{2,1},{3,4},{4,3},{5,6},{6,5},{7,8},{8,7},{9,10},{10,9},{11,... | collective-permute-start | bytes 245768 | tf_op jit(solution)/shard_map/ppermute | solution.py:289
  155.4 4.8 %collective-permute-start = (bf16[2,2,80,128]{3,2,1,0:T(8,128)(2,1)S(1)}, bf16[2,2,80,128]{3,2,1,0:T(8,128)(2,1)S(1)}, u32[]{:S(2)}, u32[]{:S(2)}) collective-permute-start(bf16[2,2,80,128]{3,2,1,0:T(8,128)(2,1)S(1)} %pad_maximum_fusion.1), channel_id=1, source_target_pairs={{0,1},{1,0},{2,3},{3,2},{4,5},{5,4},{6,7},{7,6},{8,9},{9,8},{10,11... | collective-permute-start | bytes 245768 | tf_op jit(solution)/shard_map/ppermute | solution.py:288
